TPU v7x, 32 devices: a whole 2x2x4 slice. The times are simulated.
32 devices in a mesh: row: 4 (over y, x), col: 8 (over z, core).
Axes of the slice: x: 2, y: 2, z: 4, core: 2. Of those that a mesh axis runs over, the one named last changes fastest.
Arguments:
- pair: bfloat16 [320, 320, 128], P('row', 'col'), may hold values from -6 to 6
- block_chain: int32 [5], replicated, may hold values from 0 to 1, never falling along the last dimension, each value on 1 to 4 neighbouring positions
- block_valid: int32 [5], replicated, may hold values 0 or 1
- tri_norm_gain: float32 [128], replicated, may hold values from 0.25 to 1.75
- tri_norm_bias: float32 [128], replicated, may hold values from -3 to 3
- tri_in_weight: bfloat16 [128, 512], replicated, may hold values from -0.5 to 0.5
- tri_gate_weight: bfloat16 [128, 128], replicated, may hold values from -0.5 to 0.5
- out_norm_gain: float32 [128], replicated, may hold values from 0.25 to 1.75
- out_norm_bias: float32 [128], replicated, may hold values from -3 to 3
- tri_out_weight: bfloat16 [128, 128], replicated, may hold values from -0.5 to 0.5
- att_norm_gain: float32 [128], replicated, may hold values from 0.25 to 1.75
- att_norm_bias: float32 [128], replicated, may hold values from -3 to 3
- qkvg_weight: bfloat16 [128, 512], replicated, may hold values from -0.5 to 0.5
- bias_weight: bfloat16 [128, 4], replicated, may hold values from -1 to 1
- inter_chain: float32 [4], replicated, may hold values from -3 to 3
- att_out_weight: bfloat16 [128, 128], replicated, may hold values from -0.5 to 0.5
Outputs:
- pair_out: bfloat16 [320, 320, 128], P('row', 'col')
Inputs may be any that keep to these rules, and one draw needn't show every extreme that they name: `block_chain`: chain numbers never fall along the crop; each chain covers 1 to 4 blocks and every number from 0 up appears.
All inputs are finite; a program needn't handle non-finite values.
Results may differ from a plain program's by a relative error of at most 0.0095.
Values may be sent and summed in bfloat16 or wider, within the bound.
A program may use at most 128 MiB of HBM per device.

v0:
```python
import jax
import jax.numpy as jnp
from jax import lax
from jax.sharding import PartitionSpec as P

H = 4
DH = 32
MB = 64


MASK_NEG = 10000.0
EPS = 1e-05


def layer_norm(values, gain, shift):
    middle = jnp.mean(values, axis=-1, keepdims=True)
    centred = values - middle
    spread = jnp.mean(centred * centred, axis=-1, keepdims=True)
    return centred * lax.rsqrt(spread + EPS) * gain + shift


def extra_terms(bias_part, inter_chain, key_chain, query_chain, key_valid):
    crossing = (key_chain[:, None] != query_chain[None, :]).astype(jnp.float32)
    masking = MASK_NEG * (key_valid - 1.0)
    return (
        bias_part.astype(jnp.float32)
        + inter_chain[:, None, None] * crossing[None]
        + masking[None, :, None]
    )


def attend(queries, keys, values, extra):
    scores = jnp.einsum("khd,ihd->hki", keys, queries, preferred_element_type=jnp.float32) + extra
    highest = jnp.max(scores, axis=1, keepdims=True)
    powers = jnp.exp(scores - highest)
    weights = (powers / jnp.sum(powers, axis=1, keepdims=True)).astype(jnp.bfloat16)
    return jnp.einsum("hki,khd->ihd", weights, values, preferred_element_type=jnp.float32)


def whole_bias(bias_local, row_devices, col_devices, residues):
    row_count, col_count = (bias_local.shape[0], bias_local.shape[1])
    bias_block = jnp.transpose(bias_local, (2, 0, 1))[None]
    bias_pieces = lax.all_gather(bias_block, ("row", "col"), axis=0, tiled=True)
    return (
        bias_pieces.reshape(row_devices, col_devices, H, row_count, col_count)
        .transpose(2, 0, 3, 1, 4)
        .reshape(H, residues, residues)
    )


def on_device(
    pair,
    block_chain,
    block_valid,
    tri_norm_gain,
    tri_norm_bias,
    tri_in_weight,
    tri_gate_weight,
    out_norm_gain,
    out_norm_bias,
    tri_out_weight,
    att_norm_gain,
    att_norm_bias,
    qkvg_weight,
    bias_weight,
    inter_chain,
    att_out_weight,
):
    row_count, col_count, channels = pair.shape
    hidden = tri_out_weight.shape[0]
    head_width = H * DH
    row_devices = lax.axis_size("row")
    col_devices = lax.axis_size("col")
    residues = row_count * row_devices
    row_start = lax.axis_index("row") * row_count
    col_start = lax.axis_index("col") * col_count
    residue_valid = jnp.repeat(block_valid, MB).astype(jnp.float32)
    residue_chain = jnp.repeat(block_chain, MB)
    valid_rows = lax.dynamic_slice_in_dim(residue_valid, row_start, row_count)
    valid_cols = lax.dynamic_slice_in_dim(residue_valid, col_start, col_count)
    pair_mask = (valid_rows[:, None] * valid_cols[None, :])[:, :, None]
    tri_normed = layer_norm(pair.astype(jnp.float32), tri_norm_gain, tri_norm_bias).astype(
        jnp.bfloat16
    )
    flat_normed = tri_normed.reshape(row_count * col_count, channels)
    tri_proj = jnp.dot(flat_normed, tri_in_weight, preferred_element_type=jnp.float32).reshape(
        row_count, col_count, 4 * hidden
    )
    left_side = (
        pair_mask * jax.nn.sigmoid(tri_proj[:, :, :hidden]) * tri_proj[:, :, hidden : 2 * hidden]
    ).astype(jnp.bfloat16)
    right_side = (
        pair_mask
        * jax.nn.sigmoid(tri_proj[:, :, 2 * hidden : 3 * hidden])
        * tri_proj[:, :, 3 * hidden :]
    ).astype(jnp.bfloat16)
    tri_gate = jax.nn.sigmoid(
        jnp.dot(flat_normed, tri_gate_weight, preferred_element_type=jnp.float32)
    ).reshape(row_count, col_count, channels)
    right_rows = lax.all_gather(right_side, "row", axis=0, tiled=True)
    right_cols = lax.all_to_all(right_rows, "col", split_axis=0, concat_axis=1, tiled=True)
    product = jnp.einsum(
        "ikc,jkc->ijc",
        lax.all_gather(left_side, "col", axis=1, tiled=True),
        right_cols,
        preferred_element_type=jnp.float32,
    )
    product_normed = layer_norm(product, out_norm_gain, out_norm_bias).astype(jnp.bfloat16)
    update = jnp.dot(
        product_normed.reshape(row_count * col_count, hidden),
        tri_out_weight,
        preferred_element_type=jnp.float32,
    ).reshape(row_count, col_count, channels)
    pair_mid = (pair.astype(jnp.float32) + tri_gate * update).astype(jnp.bfloat16)
    att_normed = layer_norm(pair_mid.astype(jnp.float32), att_norm_gain, att_norm_bias).astype(
        jnp.bfloat16
    )
    flat_att = att_normed.reshape(row_count * col_count, channels)
    bias_local = (
        jnp.dot(flat_att, bias_weight, preferred_element_type=jnp.float32)
        .astype(jnp.bfloat16)
        .reshape(row_count, col_count, H)
    )
    bias_full = whole_bias(bias_local, row_devices, col_devices, residues)
    bias_rows = lax.dynamic_slice_in_dim(bias_full, row_start, row_count, 2)
    projected = jnp.dot(flat_att, qkvg_weight, preferred_element_type=jnp.float32).reshape(
        row_count, col_count, 4, H, DH
    )
    queries = (projected[:, :, 0] * DH ** (-0.5)).astype(jnp.bfloat16)
    keys_vals = (
        projected[:, :, 1:3].astype(jnp.bfloat16).reshape(row_count, col_count, 2 * head_width)
    )
    gate_values = jax.nn.sigmoid(projected[:, :, 3]).reshape(row_count, col_count, head_width)
    gathered = lax.all_gather(keys_vals, "row", axis=0, tiled=True)
    chain_rows = lax.dynamic_slice_in_dim(residue_chain, row_start, row_count)
    extra_rows = extra_terms(bias_rows, inter_chain, residue_chain, chain_rows, residue_valid)
    block_cols = 8

    def one_column(query_part, key_part, value_part):
        return attend(query_part, key_part, value_part, extra_rows)

    def column_block(index):
        query_block = lax.dynamic_slice_in_dim(queries, index * block_cols, block_cols, 1)
        pair_block = lax.dynamic_slice_in_dim(gathered, index * block_cols, block_cols, 1).reshape(
            residues, block_cols, 2, H, DH
        )
        return jax.vmap(one_column, in_axes=(1, 1, 1), out_axes=1)(
            query_block, pair_block[:, :, 0], pair_block[:, :, 1]
        )

    results = lax.map(column_block, jnp.arange(col_count // block_cols))
    attended = jnp.moveaxis(results, 0, 1).reshape(row_count, col_count, head_width)
    gated_local = (gate_values * attended).astype(jnp.bfloat16)
    final_update = jnp.dot(
        gated_local.reshape(row_count * col_count, head_width),
        att_out_weight,
        preferred_element_type=jnp.float32,
    ).reshape(row_count, col_count, channels)
    return (pair_mid.astype(jnp.float32) + pair_mask * final_update).astype(jnp.bfloat16)


def solution(mesh):
    placed = (
        P("row", "col", None),
        P(),
        P(),
        P(),
        P(),
        P(),
        P(),
        P(),
        P(),
        P(),
        P(),
        P(),
        P(),
        P(),
        P(),
        P(),
    )
    return jax.shard_map(
        on_device, mesh=mesh, in_specs=placed, out_specs=P("row", "col", None), check_vma=False
    )
```

profile of v0, /device:TPU:0, one launch (start us, length us, event | category | flops | bytes accessed | tf_op | source)
XLA Modules:
  0.0 391.4 jit_solution(8317755201387593265)
XLA Ops:
  9.3 2.1 fusion.27
  14.4 1.9 fusion.33
  17.2 47.2 %all-gather.5.cloned.1.call-done = bf16[320,40,128]{2,1,0:T(8,128)(2,1)} async-done(((bf16[80,40,128]{2,1,0:T(8,128)(2,1)}), bf16[320,40,128]{2,1,0:T(8,128)(2,1)}) %all-gather.5.cloned.1.call-update) | async-done | bytes 3276816 | tf_op jit(solution)/shard_map/all_gather | solution.py:100
  64.3 4.6 %all-to-all-start = ((bf16[320,40,128]{2,1,0:T(8,128)(2,1)}), bf16[320,40,128]{2,1,0:T(8,128)(2,1)S(1)}, u32[]{:S(2)}, u32[]{:S(2)}) async-start(bf16[320,40,128]{2,1,0:T(8,128)(2,1)} %all-gather.5.cloned.1.call-done), calls=%async_computation | async-start | bytes 6553600 | tf_op jit(solution)/shard_map/all_to_all | solution.py:101
  70.0 2.9 fusion.17
  73.0 123.0 %all-to-all-done = bf16[320,40,128]{2,1,0:T(8,128)(2,1)S(1)} async-done(((bf16[320,40,128]{2,1,0:T(8,128)(2,1)}), bf16[320,40,128]{2,1,0:T(8,128)(2,1)S(1)}, u32[]{:S(2)}, u32[]{:S(2)}) %all-to-all-start) | async-done | bytes 3276832 | tf_op jit(solution)/shard_map/all_to_all | solution.py:101
  197.6 2.8 copy.79
  200.5 4.5 %copy.80 = bf16[40,320,128]{1,0,2:T(8,128)(2,1)} copy(bf16[40,320,128]{2,1,0:T(8,128)(2,1)S(1)} %bitcast.91) | data formatting | bytes 6553600 | tf_op jit(solution)/shard_map/all_to_all | solution.py:101
  204.9 14.4 %copy.81 = bf16[80,320,128]{0,1,2:T(8,128)(2,1)} copy(bf16[80,320,128]{2,1,0:T(8,128)(2,1)} %all-gather.7.cloned.1.call-done) | data formatting | bytes 13107200 | tf_op jit(solution)/shard_map/all_gather | solution.py:104
  219.4 7.3 %bitcast_reduce_fusion = (f32[80,40]{0,1:T(8,128)S(1)}, f32[128,40,80]{2,1,0:T(8,128)S(1)}) fusion(bf16[40,320,128]{1,0,2:T(8,128)(2,1)} %copy.80, bf16[80,320,128]{0,1,2:T(8,128)(2,1)} %copy.81), kind=kOutput, calls=%fused_computation.29 | convolution fusion | flops 262550400 | bytes 11481600 | tf_op jit(solution)/shard_map/ikc,jkc->ijc/dot_general | solution.py:102
  229.1 2.5 copy.86
  231.6 2.1 convert_reduce_fusion
  236.7 8.5 %fusion.43 = f32[80,40,4,4,32]{1,4,3,2,0:T(8,128)} fusion(bf16[4,4,32,128,1]{3,2,1,0,4:T(8,128)(2,1)S(1)} %bitcast.97, bf16[80,40,128]{2,1,0:T(8,128)(2,1)S(1)} %fusion.26), kind=kOutput, calls=%fused_computation.67 | convolution fusion | flops 419430400 | bytes 7503872 | tf_op jit(solution)/shard_map/dot_general | solution.py:126
  245.3 7.8 %slice.89 = bf16[80,40,2,4,32]{1,4,3,2,0:T(8,128)(2,1)} slice(f32[80,40,4,4,32]{1,4,3,2,0:T(8,128)} %fusion.43), slice={[0:80], [0:40], [1:3], [0:4], [0:32]} | slice | bytes 3276800 | tf_op jit(solution)/shard_map/slice | solution.py:131
  253.0 5.8 %copy.88 = bf16[80,40,256]{2,1,0:T(8,128)(2,1)} copy(bf16[80,40,256]{1,2,0:T(8,128)(2,1)} %bitcast.89) | data formatting | bytes 3276800 | tf_op jit(solution)/shard_map/reshape | solution.py:131
  259.8 6.7 %fusion.18 = (bf16[80,40,4,32]{1,3,2,0:T(8,128)(2,1)S(1)}, f32[80,40,1,4,32]{1,4,3,2,0:T(8,128)}) fusion(f32[80,40,4,4,32]{1,4,3,2,0:T(8,128)} %fusion.43), kind=kLoop, calls=%fused_computation.27 | loop fusion | flops 2048000 | bytes 5734400 | tf_op jit(solution)/shard_map/convert_element_type | solution.py:129
  266.5 4.7 %copy.92 = bf16[80,40,4,32]{0,3,2,1:T(8,128)(2,1)} copy(bf16[80,40,4,32]{1,3,2,0:T(8,128)(2,1)S(1)} %get-tuple-element.82) | data formatting | bytes 1638400 | tf_op jit(solution)/shard_map/while | solution.py:151
  272.9 44.9 %all-gather = bf16[128,80,40]{1,2,0:T(8,128)(2,1)S(1)} all-gather(bf16[4,80,40]{1,2,0:T(8,128)(2,1)S(1)} %copy.89), channel_id=2, replica_groups=mesh['row'=4,'col'=8] {'row','col'}, dimensions={0}, use_global_device_ids=true | all-gather | bytes 844800 | tf_op jit(solution)/shard_map/all_gather | solution.py:43
  319.8 5.2 %copy.93 = f32[80,40,128]{2,1,0:T(8,128)} copy(f32[80,40,128]{1,2,0:T(8,128)} %bitcast.90) | data formatting | bytes 3276800 | tf_op jit(solution)/shard_map/div | solution.py:133
  325.1 10.0 %all-gather.9.cloned.1.call-done = bf16[320,40,256]{2,1,0:T(8,128)(2,1)} async-done(((bf16[80,40,256]{2,1,0:T(8,128)(2,1)}), bf16[320,40,256]{2,1,0:T(8,128)(2,1)}) %all-gather.9.cloned.1.call-update) | async-done | bytes 6553616 | tf_op jit(solution)/shard_map/all_gather | solution.py:134
  335.1 44.3 %while.10 = (s32[]{:T(128)}, f32[5,80,8,4,32]{1,4,3,2,0:T(8,128)}, s32[5]{0:T(128)S(1)}, bf16[320,40,256]{2,1,0:T(8,128)(2,1)}, bf16[80,40,4,32]{0,3,2,1:T(8,128...) while((s32[]{:T(128)}, f32[5,80,8,4,32]{1,4,3,2,0:T(8,128)}, ...), condition=%wide.region_9.10_spmd, body=%wide.region_6.9_spmd.sunk | while | flops 109773120 | bytes 21801640 | solution.py:151
  377.6 1.7 fusion.66
  379.4 2.5 copy.94
  381.9 2.9 fusion.32
  (115 shorter events, 58.7 us)
Async XLA Ops:
  6.5 6.9 %copy-start = (bf16[128,512]{1,0:T(8,128)(2,1)S(1)}, bf16[128,512]{1,0:T(8,128)(2,1)}, u32[]{:S(2)}) copy-start(bf16[128,512]{1,0:T(8,128)(2,1)} %param.23) | copy-start | bytes 393220
  6.5 4.9 %copy-start.5 = (bf16[80,40,128]{2,1,0:T(8,128)(2,1)S(1)}, bf16[80,40,128]{2,1,0:T(8,128)(2,1)}, u32[]{:S(2)}) copy-start(bf16[80,40,128]{2,1,0:T(8,128)(2,1)} %param.18) | copy-start | bytes 2457604
  6.5 4.9 %copy-start.13 = (f32[128]{0:T(128)S(1)}, f32[128]{0:T(128)}, u32[]{:S(2)}) copy-start(f32[128]{0:T(128)} %param.21) | copy-start | bytes 1540
  6.5 4.9 %copy-start.12 = (f32[128]{0:T(128)S(1)}, f32[128]{0:T(128)}, u32[]{:S(2)}) copy-start(f32[128]{0:T(128)} %param.22) | copy-start | bytes 1540
  6.5 57.8 %all-gather.5.cloned.1.call-start = ((), (), s32[]{:S(2)}) async-start(), calls=%async_computation.1 | async-start | bytes 4096000 | tf_op jit(solution)/shard_map/all_gather | solution.py:100
  12.5 0.9 copy-start.8
  16.4 188.5 %all-gather.7.cloned.1.call-start = ((), (), s32[]{:S(2)}) async-start(), calls=%async_computation.2 | async-start | bytes 7372800 | tf_op jit(solution)/shard_map/all_gather | solution.py:104
  17.2 52.9 %copy-start.20 = (bf16[128,128]{1,0:T(8,128)(2,1)S(1)}, bf16[128,128]{1,0:T(8,128)(2,1)}, u32[]{:S(2)}) copy-start(bf16[128,128]{1,0:T(8,128)(2,1)} %param.24) | copy-start | bytes 98308
  64.3 131.6 %all-to-all-start = ((bf16[320,40,128]{2,1,0:T(8,128)(2,1)}), bf16[320,40,128]{2,1,0:T(8,128)(2,1)S(1)}, u32[]{:S(2)}, u32[]{:S(2)}) async-start(bf16[320,40,128]{2,1,0:T(8,128)(2,1)} %all-gather.5.cloned.1.call-done), calls=%async_computation | async-start | bytes 6553600 | tf_op jit(solution)/shard_map/all_to_all | solution.py:101
  68.9 266.2 %all-gather.9.cloned.1.call-start = ((), (), s32[]{:S(2)}) async-start(), calls=%async_computation.3 | async-start | bytes 8192000 | tf_op jit(solution)/shard_map/all_gather | solution.py:134
  195.9 1.7 copy-start.2
  226.7 0.8 copy-start.14
  226.7 0.8 copy-start.15
  229.0 2.5 copy-start.6
  229.1 2.6 copy-start.9
  231.6 3.1 copy-start.16
  231.6 3.1 copy-start.17
  233.7 1.0 copy-start.3
  235.8 0.9 copy-start.7
  266.5 4.7 %copy-start.11 = (bf16[128,4]{0,1:T(4,128)(2,1)S(1)}, bf16[128,4]{0,1:T(4,128)(2,1)}, u32[]{:S(2)}) copy-start(bf16[128,4]{0,1:T(4,128)(2,1)} %param.31) | copy-start | bytes 3076
  319.7 5.2 %copy-start.19 = (f32[4]{0:T(128)S(1)}, f32[4]{0:T(128)}, u32[]{:S(2)}) copy-start(f32[4]{0:T(128)} %param.32) | copy-start | bytes 52
  379.4 2.6 copy-start.4
  379.4 2.6 copy-start.10
  379.4 5.5 %copy-start.1 = (bf16[128,512]{1,0:T(8,128)(2,1)S(1)}, bf16[128,512]{1,0:T(8,128)(2,1)}, u32[]{:S(2)}) copy-start(bf16[128,512]{1,0:T(8,128)(2,1)} %param.23) | copy-start | bytes 393220
  (1 other events, 0.7 us)
Sparse Core Ops, SparseCore 0:
  16.5 47.7 all-gather.4
  65.9 125.6 all-gather.6
  259.0 76.0 all-gather.8
where the time goes:
time: 393 us; the launch traced here: 391 us
  waiting for transfers between devices  181 us (46%)
  local copies, waits for them, and re-layouts  74.2 us (19%)
  blocking collectives  44.9 us (11%)
  matrix products  43.2 us (11%)
  other arithmetic  26.9 us (7%)
  between operations  13.5 us (3%)
  starting transfers between devices  4.72 us (1%)
    all_to_all x1, waiting for transfers between devices, on_device(): lax.all_to_all(right_rows, 'col', split_axis=0, concat_axis=1, tiled=True)  123 us
    all_gather x1, waiting for transfers between devices, on_device(): right_rows = lax.all_gather(right_side, 'row', axis=0, tiled=True)  47.2 us
    all_gather x1, blocking collectives, whole_bias(): bias_pieces = lax.all_gather(bias_block, ('row', 'col'), axis=0, tiled=True)  44.9 us
    all_gather x1, local copies, waits for them, and re-layouts, on_device(): lax.all_gather(left_side, 'col', axis=1, tiled=True)  14.4 us
    dynamic_slice x10, local copies, waits for them, and re-layouts, column_block(): lax.dynamic_slice_in_dim(gathered, index * block_cols, block_cols, 1)  12.8 us
    all_gather x1, waiting for transfers between devices, on_device(): gathered = lax.all_gather(keys_vals, 'row', axis=0, tiled=True)  9.99 us
    dot_general x5, matrix products, attend(): jnp.einsum('hki,khd->ihd', weights, values, preferred_element_type=jnp.fl...  8.6 us
    dot_general x1, matrix products, on_device(): jnp.dot(flat_att, qkvg_weight, preferred_element_type=jnp.float32)  8.54 us
  transfers between devices with their start and end apart: 4, of which 3 were waited for; matrix products, arithmetic and copies ran while one was open for 8% of the time, Pallas kernels for 0%

commit v1 on v0

v1 whole, which is shorter than its diff:
```python
import functools

import jax
import jax.numpy as jnp
from jax import lax
from jax.experimental import pallas as pl
from jax.experimental.pallas import tpu as pltpu
from jax.sharding import PartitionSpec as P

H = 4
DH = 32
MB = 64

MASK_NEG = 10000.0
EPS = 1e-05
F32 = jnp.float32
BF16 = jnp.bfloat16
VMEM_LIMIT = 48 * 1024 * 1024


def layer_norm(values, gain, shift, axis=-1):
    middle = jnp.mean(values, axis=axis, keepdims=True)
    centred = values - middle
    spread = jnp.mean(centred * centred, axis=axis, keepdims=True)
    return centred * lax.rsqrt(spread + EPS) * gain + shift


def dot_nt(left, right):
    return lax.dot_general(left, right, (((1,), (1,)), ((), ())), preferred_element_type=F32)


def dot_tn(left, right):
    return lax.dot_general(left, right, (((0,), (0,)), ((), ())), preferred_element_type=F32)


def dot_nn(left, right):
    return lax.dot_general(left, right, (((1,), (0,)), ((), ())), preferred_element_type=F32)


def project_kernel(
    pair_ref, valid_i_ref, valid_j_ref, gain_ref, shift_ref, in_t_ref, gate_w_ref, sides_ref, gate_ref
):
    hidden = sides_ref.shape[2]
    normed = layer_norm(pair_ref[0].astype(F32), gain_ref[...], shift_ref[...]).astype(BF16)
    proj = dot_nt(in_t_ref[...], normed)
    mask = valid_i_ref[...] * valid_j_ref[0]
    sides_ref[0, 0] = (mask * jax.nn.sigmoid(proj[:hidden]) * proj[hidden : 2 * hidden]).astype(BF16)
    sides_ref[0, 1] = (
        mask * jax.nn.sigmoid(proj[2 * hidden : 3 * hidden]) * proj[3 * hidden :]
    ).astype(BF16)
    gate_ref[0] = jax.nn.sigmoid(dot_nn(normed, gate_w_ref[...]))


def middle_kernel(
    pair_ref,
    product_ref,
    gate_ref,
    out_gain_ref,
    out_shift_ref,
    out_w_ref,
    att_gain_ref,
    att_shift_ref,
    bias_t_ref,
    mid_ref,
    bias_ref,
):
    normed = layer_norm(
        product_ref[0].astype(F32), out_gain_ref[...], out_shift_ref[...], axis=0
    ).astype(BF16)
    update = dot_tn(normed, out_w_ref[...])
    mid = (pair_ref[0].astype(F32) + gate_ref[0] * update).astype(BF16)
    mid_ref[0] = mid
    att = layer_norm(mid.astype(F32), att_gain_ref[...], att_shift_ref[...]).astype(BF16)
    bias_ref[0] = dot_nt(bias_t_ref[...], att).astype(BF16)


def attention_kernel(
    mid_ref,
    extra_ref,
    valid_i_ref,
    valid_j_ref,
    gain_ref,
    shift_ref,
    qkvg_ref,
    out_w_ref,
    result_ref,
):
    width = H * DH
    mid = mid_ref[0].astype(F32)
    att = layer_norm(mid, gain_ref[...], shift_ref[...]).astype(BF16)
    heads = dot_nn(att, qkvg_ref[...])
    queries = (heads[:, :width] * DH ** (-0.5)).astype(BF16)
    keys = heads[:, width : 2 * width].astype(BF16)
    vals = heads[:, 2 * width : 3 * width].astype(BF16)
    gate = jax.nn.sigmoid(heads[:, 3 * width :])
    attended = []
    for head in range(H):
        lanes = slice(head * DH, (head + 1) * DH)
        scores = dot_nt(queries[:, lanes], keys[:, lanes]) + extra_ref[head]
        powers = jnp.exp(scores - jnp.max(scores, axis=1, keepdims=True))
        total = jnp.sum(powers, axis=1, keepdims=True)
        attended.append(dot_nn(powers.astype(BF16), vals[:, lanes]) / total)
    gated = (gate * jnp.concatenate(attended, axis=1)).astype(BF16)
    update = dot_nn(gated, out_w_ref[...])
    mask = valid_i_ref[...] * valid_j_ref[0]
    result_ref[0] = (mid + mask * update).astype(BF16)


def whole(shape):
    return pl.BlockSpec(shape, lambda c: (0,) * len(shape))


def per_column(shape):
    return pl.BlockSpec((1,) + shape, lambda c: (c,) + (0,) * len(shape))


def column_call(kernel, columns, ins, outs):
    return pl.pallas_call(
        kernel,
        grid=(columns,),
        in_specs=[per_column(a.shape[1:]) if cut else whole(a.shape) for a, cut in ins],
        out_specs=[per_column(shape) for shape, _ in outs],
        out_shape=[jax.ShapeDtypeStruct((columns,) + shape, t) for shape, t in outs],
        compiler_params=pltpu.CompilerParams(vmem_limit_bytes=VMEM_LIMIT),
    )(*[a for a, _ in ins])


def on_device(
    pair,
    block_chain,
    block_valid,
    tri_norm_gain,
    tri_norm_bias,
    tri_in_weight,
    tri_gate_weight,
    out_norm_gain,
    out_norm_bias,
    tri_out_weight,
    att_norm_gain,
    att_norm_bias,
    qkvg_weight,
    bias_weight,
    inter_chain,
    att_out_weight,
):
    row_count, col_count, channels = pair.shape
    hidden = tri_out_weight.shape[0]
    row_devices = lax.axis_size("row")
    residues = row_count * row_devices
    strip = col_count // row_devices
    axes = ("col", "row")
    residue_valid = jnp.repeat(block_valid, MB).astype(F32)
    residue_chain = jnp.repeat(block_chain, MB)
    strip_start = lax.axis_index("col") * col_count + lax.axis_index("row") * strip
    valid_j = lax.dynamic_slice_in_dim(residue_valid, strip_start, strip)[:, None, None]

    own = lax.all_to_all(jnp.swapaxes(pair, 0, 1), "row", split_axis=0, concat_axis=1, tiled=True)
    sides, tri_gate = column_call(
        project_kernel,
        strip,
        [
            (own, True),
            (residue_valid[None, :], False),
            (valid_j, True),
            (tri_norm_gain[None, :], False),
            (tri_norm_bias[None, :], False),
            (tri_in_weight.T, False),
            (tri_gate_weight, False),
        ],
        [((2, hidden, residues), BF16), ((residues, channels), F32)],
    )
    spread = lax.all_to_all(sides, axes, split_axis=2, concat_axis=0, tiled=True)
    product = jnp.einsum(
        "kci,kcj->cji", spread[:, 0], spread[:, 1], preferred_element_type=F32
    ).astype(BF16)
    product = lax.all_to_all(product, axes, split_axis=1, concat_axis=0, tiled=True)
    mid, bias = column_call(
        middle_kernel,
        strip,
        [
            (own, True),
            (jnp.swapaxes(product, 0, 1), True),
            (tri_gate, True),
            (out_norm_gain[:, None], False),
            (out_norm_bias[:, None], False),
            (tri_out_weight, False),
            (att_norm_gain[None, :], False),
            (att_norm_bias[None, :], False),
            (bias_weight.T, False),
        ],
        [((residues, channels), BF16), ((H, residues), BF16)],
    )
    bias = lax.all_gather(bias, axes, axis=0, tiled=True)
    crossing = (residue_chain[:, None] != residue_chain[None, :]).astype(F32)
    extra = (
        jnp.swapaxes(bias, 0, 1).astype(F32)
        + inter_chain[:, None, None] * crossing[None]
        + (MASK_NEG * (residue_valid - 1.0))[None, None, :]
    )
    (result,) = column_call(
        attention_kernel,
        strip,
        [
            (mid, True),
            (extra, False),
            (residue_valid[:, None], False),
            (valid_j, True),
            (att_norm_gain[None, :], False),
            (att_norm_bias[None, :], False),
            (qkvg_weight, False),
            (att_out_weight, False),
        ],
        [((residues, channels), BF16)],
    )
    result = lax.all_to_all(result, "row", split_axis=1, concat_axis=0, tiled=True)
    return jnp.swapaxes(result, 0, 1)


def solution(mesh):
    placed = (P("row", "col", None),) + (P(),) * 15
    return jax.shard_map(
        on_device, mesh=mesh, in_specs=placed, out_specs=P("row", "col", None), check_vma=False
    )
```

time: 393 us -> 237 us (0.60)
  waiting for transfers between devices: 181 us -> 32.5 us
  blocking collectives: 44.9 us -> 138 us
  local copies, waits for them, and re-layouts: 74.2 us -> 20.3 us
  matrix products: 43.2 us -> 2.25 us
  Pallas kernels: 0 us -> 32.6 us
  other arithmetic: 26.9 us -> 1.76 us
  between operations: 13.5 us -> 0.22 us
    all_to_all x1 -> x2, waiting for transfers between devices: 123 us -> 32.5 us  [the longest x1 21.9 us: on_device(): lax.all_to_all(product, axes, split_axis=1, concat_axis=0, tiled=True)]
    all_to_all x0 -> x2, blocking collectives: none -> 66.4 us  [the longest x1 51.1 us: on_device(): lax.all_to_all(sides, axes, split_axis=2, concat_axis=0, tiled=True)]
    all_gather x3 -> x0, waiting for transfers between devices: 57.1 us -> none  [the longest x1 47.2 us: on_device(): right_rows = lax.all_gather(right_side, 'row', axis=0, tiled=True)]
    dot_general x17 -> x1, matrix products: 43.2 us -> 2.25 us  [on_device(): jnp.einsum('kci,kcj->cji', spread[:, 0], spread[:, 1], preferred_element_...]
    pallas_call x0 -> x3, Pallas kernels: none -> 32.6 us  [column_call(): pl.pallas_call(kernel, grid=(columns,), in_specs=[per_column(a.shape[1:])...]
    all_gather x1, blocking collectives: 44.9 us -> 71.7 us  [on_device(): bias = lax.all_gather(bias, axes, axis=0, tiled=True)]
    dynamic_slice x18 -> x0, local copies, waits for them, and re-layouts: 16 us -> none  [the longest x10 12.8 us: column_block(): lax.dynamic_slice_in_dim(gathered, index * block_cols, block_cols, 1)]
    all_gather x1 -> x0, local copies, waits for them, and re-layouts: 14.4 us -> none  [on_device(): lax.all_gather(left_side, 'col', axis=1, tiled=True)]
  transfers between devices with their start and end apart: 4 -> 2, of which waited for: 3 -> 2; matrix products, arithmetic and copies ran while one was open for 8% -> 2% of each run, Pallas kernels for 0% -> 0%
where the time goes in v1:
time: 237 us; the launch traced here: 236 us
  blocking collectives  138 us (58%)
  Pallas kernels  32.6 us (14%)
  waiting for transfers between devices  32.5 us (14%)
  local copies, waits for them, and re-layouts  20.3 us (9%)
  starting transfers between devices  8.41 us (4%)
    all_gather x1, blocking collectives, on_device(): bias = lax.all_gather(bias, axes, axis=0, tiled=True)  71.7 us
    all_to_all x1, blocking collectives, on_device(): lax.all_to_all(sides, axes, split_axis=2, concat_axis=0, tiled=True)  51.1 us
    pallas_call x3, Pallas kernels, column_call(): pl.pallas_call(kernel, grid=(columns,), in_specs=[per_column(a.shape[1:])...  32.6 us
    all_to_all x1, waiting for transfers between devices, on_device(): lax.all_to_all(product, axes, split_axis=1, concat_axis=0, tiled=True)  21.9 us
    all_to_all x1, blocking collectives, on_device(): lax.all_to_all(result, 'row', split_axis=1, concat_axis=0, tiled=True)  15.3 us
    all_to_all x1, waiting for transfers between devices, on_device(): lax.all_to_all(jnp.swapaxes(pair, 0, 1), 'row', split_axis=0, concat_axis...  10.6 us
    unnamed x41, local copies, waits for them, and re-layouts  6.62 us
    all_to_all x1, starting transfers between devices, on_device(): lax.all_to_all(jnp.swapaxes(pair, 0, 1), 'row', split_axis=0, concat_axis...  5.29 us
  transfers between devices with their start and end apart: 2, of which 2 were waited for; matrix products, arithmetic and copies ran while one was open for 2% of the time, Pallas kernels for 0%

profile of v1, /device:TPU:0, one launch (start us, length us, event | category | flops | bytes accessed | tf_op | source)
XLA Modules:
  0.0 236.1 jit_solution(6725745297855597788)
XLA Ops:
  0.0 2.2 copy.91
  2.2 5.3 %all-to-all-start = ((bf16[40,80,128]{2,1,0:T(8,128)(2,1)}), bf16[40,80,128]{2,1,0:T(8,128)(2,1)S(1)}, u32[]{:S(2)}, u32[]{:S(2)}) async-start(bf16[40,80,128]{2,1,0:T(8,128)(2,1)} %bitcast.42), calls=%async_computation | async-start | bytes 1638400 | tf_op jit(solution)/shard_map/all_to_all | solution.py:157
  8.0 10.6 %all-to-all-done = bf16[40,80,128]{2,1,0:T(8,128)(2,1)S(1)} async-done(((bf16[40,80,128]{2,1,0:T(8,128)(2,1)}), bf16[40,80,128]{2,1,0:T(8,128)(2,1)S(1)}, u32[]{:S(2)}, u32[]{:S(2)}) %all-to-all-start) | async-done | bytes 819232 | tf_op jit(solution)/shard_map/all_to_all | solution.py:157
  18.8 4.7 %shard_map.154 = (bf16[10,2,128,320]{3,2,1,0:T(8,128)(2,1)S(1)}, f32[10,320,128]{2,1,0:T(8,128)S(1)}) custom-call(bf16[10,320,128]{2,1,0:T(8,128)(2,1)S(1)} %bitcast.43, f32[1,320]{1,0:T(1,128)S(1)} %convert_element_type.50.valid_i_ref, f32[10,1,1]{2,1,0:T(1,128)S(1)} %copy.66.valid_j_ref, f32[1,128]{1,0:T(1,128)S(1)} %bitcast.52, f32[1,128]{1,0:T(1,128)S(1)} %bitcast.53, ...), custom_call_target="tpu_custom_call" | custom-call | tf_op jit(solution)/shard_map/pallas_call | solution.py:118
  23.5 2.0 copy.67
  25.5 51.1 %all_to_all.72 = bf16[10,2,128,320]{3,1,0,2:T(2,128)(2,1)S(1)} all-to-all(bf16[10,2,128,320]{3,1,0,2:T(2,128)(2,1)S(1)} %copy.67), channel_id=1, replica_groups=mesh['row'=4,'col'=8] {'col','row'}, dimensions={2} | all-to-all | bytes 3276800 | tf_op jit(solution)/shard_map/all_to_all | solution.py:172
  76.6 1.0 copy.69
  77.6 1.6 fusion.2
  79.3 2.1 copy.85
  81.4 2.3 convolution_convert_fusion
  83.7 1.7 copy.72
  85.4 3.1 %all-to-all-start.2 = ((bf16[4,320,320]{2,0,1:T(4,128)(2,1)}), bf16[4,320,320]{2,0,1:T(4,128)(2,1)S(1)}, u32[]{:S(2)}, u32[]{:S(2)}) async-start(bf16[4,320,320]{2,0,1:T(4,128)(2,1)} %copy.72), calls=%async_computation.2 | async-start | bytes 1966080 | tf_op jit(solution)/shard_map/all_to_all | solution.py:176
  88.5 0.8 convert_element_type.58.valid_i_ref
  89.5 0.7 copy.75.out_shift_ref
  90.9 0.9 compare_convert_fusion
  91.8 21.9 %all-to-all-done.2 = bf16[4,320,320]{2,0,1:T(4,128)(2,1)S(1)} async-done(((bf16[4,320,320]{2,0,1:T(4,128)(2,1)}), bf16[4,320,320]{2,0,1:T(4,128)(2,1)S(1)}, u32[]{:S(2)}, u32[]{:S(2)}) %all-to-all-start.2) | async-done | bytes 819232 | tf_op jit(solution)/shard_map/all_to_all | solution.py:176
  113.7 1.4 copy.73
  115.1 1.7 all_to_all.63
  116.8 0.8 copy-done.1
  118.3 6.5 %shard_map.155 = (bf16[10,320,128]{2,1,0:T(8,128)(2,1)S(1)}, bf16[10,4,320]{2,1,0:T(4,128)(2,1)S(1)}) custom-call(bf16[10,320,128]{2,1,0:T(8,128)(2,1)S(1)} %bitcast.44, bf16[10,128,320]{2,1,0:T(8,128)(2,1)S(1)} %bitcast.45, f32[10,320,128]{2,1,0:T(8,128)S(1)} %get-tuple-element.10.gate_ref, f32[128,1]{1,0:T(8,128)S(1)} %copy.74.out_gain_ref, ...), custom_call_target="tpu_custom_call" | custom-call | tf_op jit(solution)/shard_map/pallas_call | solution.py:118
  124.8 71.7 %all_gather.3 = bf16[320,4,320]{2,1,0:T(4,128)(2,1)S(1)} all-gather(bf16[10,4,320]{2,1,0:T(4,128)(2,1)S(1)} %get-tuple-element.12), channel_id=1, replica_groups=mesh['row'=4,'col'=8] {'col','row'}, dimensions={0}, use_global_device_ids=true | all-gather | bytes 844800 | tf_op jit(solution)/shard_map/all_gather | solution.py:193
  197.5 21.3 %shard_map.156 = bf16[10,320,128]{2,1,0:T(8,128)(2,1)S(1)} custom-call(bf16[10,320,128]{2,1,0:T(8,128)(2,1)S(1)} %get-tuple-element.11.mid_ref, f32[4,320,320]{2,1,0:T(8,128)S(1)} %fusion.extra_ref, f32[320,1]{1,0:T(8,128)S(1)} %copy-done, f32[10,1,1]{2,1,0:T(1,128)S(1)} %copy.66.valid_j_ref, f32[1,128]{1,0:T(1,128)S(1)} %bitcast.48, f32[1,128]{1,0:T(1,128)S(1)} %bitcast.50, ...), custom_call_target="tpu_custom_call" | custom-call | tf_op jit(solution)/shard_map/pallas_call | solution.py:118
  219.5 15.3 %all_to_all.73 = bf16[10,320,128]{2,0,1:T(8,128)(2,1)S(1)} all-to-all(bf16[10,320,128]{2,0,1:T(8,128)(2,1)S(1)} %copy.79), channel_id=1, replica_groups=mesh['row'=4,'col'=8] {'row'}, dimensions={1} | all-to-all | bytes 1638400 | tf_op jit(solution)/shard_map/all_to_all | solution.py:215
  235.0 1.1 copy.82
  (52 shorter events, 3.9 us)
Async XLA Ops:
  0.0 7.5 %copy-start.18 = (s32[5]{0:T(128)S(1)}, s32[5]{0:T(128)}, u32[]{:S(2)}) copy-start(s32[5]{0:T(128)} %param.18) | copy-start | bytes 64
  0.0 7.9 %copy-start.12 = (bf16[128,512]{1,0:T(8,128)(2,1)S(1)}, bf16[128,512]{1,0:T(8,128)(2,1)}, u32[]{:S(2)}) copy-start(bf16[128,512]{1,0:T(8,128)(2,1)} %param.21) | copy-start | bytes 393220
  2.2 16.5 %copy-start.5 = (bf16[128,128]{1,0:T(8,128)(2,1)S(1)}, bf16[128,128]{1,0:T(8,128)(2,1)}, u32[]{:S(2)}) copy-start(bf16[128,128]{1,0:T(8,128)(2,1)} %gate_w_ref.1) | copy-start | bytes 98308
  2.2 16.6 %copy-start.9 = (f32[128]{0:T(128)S(1)}, f32[128]{0:T(128)}, u32[]{:S(2)}) copy-start(f32[128]{0:T(128)} %param.19) | copy-start | bytes 1540
  2.2 16.6 %copy-start.10 = (f32[128]{0:T(128)S(1)}, f32[128]{0:T(128)}, u32[]{:S(2)}) copy-start(f32[128]{0:T(128)} %param.20) | copy-start | bytes 1540
  2.2 16.5 %all-to-all-start = ((bf16[40,80,128]{2,1,0:T(8,128)(2,1)}), bf16[40,80,128]{2,1,0:T(8,128)(2,1)S(1)}, u32[]{:S(2)}, u32[]{:S(2)}) async-start(bf16[40,80,128]{2,1,0:T(8,128)(2,1)} %bitcast.42), calls=%async_computation | async-start | bytes 1638400 | tf_op jit(solution)/shard_map/all_to_all | solution.py:157
  83.6 5.7 %copy-start.14 = (f32[128]{0:T(128)S(1)}, f32[128]{0:T(128)}, u32[]{:S(2)}) copy-start(f32[128]{0:T(128)} %param.23) | copy-start | bytes 1540
  83.6 5.8 %copy-start.15 = (f32[128]{0:T(128)S(1)}, f32[128]{0:T(128)}, u32[]{:S(2)}) copy-start(f32[128]{0:T(128)} %param.24) | copy-start | bytes 1540
  83.6 6.5 %copy-start.17 = (s32[5]{0:T(128)S(1)}, s32[5]{0:T(128)}, u32[]{:S(2)}) copy-start(s32[5]{0:T(128)} %param.17) | copy-start | bytes 64
  85.4 28.3 %all-to-all-start.2 = ((bf16[4,320,320]{2,0,1:T(4,128)(2,1)}), bf16[4,320,320]{2,0,1:T(4,128)(2,1)S(1)}, u32[]{:S(2)}, u32[]{:S(2)}) async-start(bf16[4,320,320]{2,0,1:T(4,128)(2,1)} %copy.72), calls=%async_computation.2 | async-start | bytes 1966080 | tf_op jit(solution)/shard_map/all_to_all | solution.py:176
  113.7 3.1 %copy-start.3 = (bf16[128,128]{1,0:T(8,128)(2,1)S(1)}, bf16[128,128]{1,0:T(8,128)(2,1)}, u32[]{:S(2)}) copy-start(bf16[128,128]{1,0:T(8,128)(2,1)} %out_w_ref.2) | copy-start | bytes 98308
  113.7 3.1 %copy-start.6 = (f32[128]{0:T(128)S(1)}, f32[128]{0:T(128)}, u32[]{:S(2)}) copy-start(f32[128]{0:T(128)} %param.26) | copy-start | bytes 1540
  113.7 3.1 %copy-start.7 = (f32[128]{0:T(128)S(1)}, f32[128]{0:T(128)}, u32[]{:S(2)}) copy-start(f32[128]{0:T(128)} %param.27) | copy-start | bytes 1540
  116.8 0.8 copy-start.1
  117.6 0.7 copy-start.8
  118.3 78.2 %copy-start.11 = (f32[320,320]{1,0:T(8,128)S(1)}, f32[320,320]{1,0:T(8,128)}, u32[]{:S(2)}) copy-start(f32[320,320]{1,0:T(8,128)} %compare_convert_fusion) | copy-start | bytes 1228804
  118.3 78.2 %copy-start.13 = (f32[320]{0:T(512)S(1)}, f32[320]{0:T(512)}, u32[]{:S(2)}) copy-start(f32[320]{0:T(512)} %add_multiply_fusion) | copy-start | bytes 3844
  118.3 78.2 %copy-start.16 = (f32[4]{0:T(128)S(1)}, f32[4]{0:T(128)}, u32[]{:S(2)}) copy-start(f32[4]{0:T(128)} %param.30) | copy-start | bytes 52
  196.5 0.9 copy-start
  196.6 1.0 copy-start.2
  196.6 1.0 copy-start.4

commit v2 on v1

v2 whole, which is shorter than its diff:
```python
import functools

import jax
import jax.numpy as jnp
from jax import lax
from jax.experimental import pallas as pl
from jax.experimental.pallas import tpu as pltpu
from jax.sharding import PartitionSpec as P

H = 4
DH = 32
MB = 64

MASK_NEG = 10000.0
EPS = 1e-05
F32 = jnp.float32
BF16 = jnp.bfloat16
MESH = pl.DeviceIdType.MESH
VMEM_LIMIT = 48 * 1024 * 1024


def layer_norm(values, gain, shift, axis=-1):
    middle = jnp.mean(values, axis=axis, keepdims=True)
    centred = values - middle
    spread = jnp.mean(centred * centred, axis=axis, keepdims=True)
    return centred * lax.rsqrt(spread + EPS) * gain + shift


def dot_nt(left, right):
    return lax.dot_general(left, right, (((1,), (1,)), ((), ())), preferred_element_type=F32)


def dot_tn(left, right):
    return lax.dot_general(left, right, (((0,), (0,)), ((), ())), preferred_element_type=F32)


def dot_nn(left, right):
    return lax.dot_general(left, right, (((1,), (0,)), ((), ())), preferred_element_type=F32)


def project_kernel(pair_ref, mask_ref, gain_ref, shift_ref, in_t_ref, gate_w_ref, sides_ref, gate_ref):
    columns, rows, channels = pair_ref.shape
    flat = pair_ref[...].reshape(columns * rows, channels).astype(F32)
    normed = layer_norm(flat, gain_ref[...], shift_ref[...]).astype(BF16)
    proj = dot_nt(in_t_ref[...], normed)
    half = sides_ref.shape[0]
    sides_ref[...] = (mask_ref[...] * jax.nn.sigmoid(proj[:half]) * proj[half:]).astype(BF16)
    gate = jax.nn.sigmoid(dot_nn(normed, gate_w_ref[...]))
    gate_ref[...] = gate.reshape(columns, rows, channels)


def middle_kernel(
    pair_ref,
    product_ref,
    gate_ref,
    out_gain_ref,
    out_shift_ref,
    out_w_ref,
    att_gain_ref,
    att_shift_ref,
    bias_t_ref,
    mid_ref,
    bias_ref,
):
    columns, rows, channels = pair_ref.shape
    normed = layer_norm(
        product_ref[...].astype(F32), out_gain_ref[...], out_shift_ref[...], axis=0
    ).astype(BF16)
    update = dot_tn(normed, out_w_ref[...])
    flat = pair_ref[...].reshape(columns * rows, channels).astype(F32)
    mid = (flat + gate_ref[...].reshape(columns * rows, channels) * update).astype(BF16)
    mid_ref[...] = mid.reshape(columns, rows, channels)
    att = layer_norm(mid.astype(F32), att_gain_ref[...], att_shift_ref[...]).astype(BF16)
    bias_ref[...] = dot_nt(bias_t_ref[...], att).astype(BF16)


def attention_kernel(
    mid_ref,
    extra_ref,
    valid_i_ref,
    valid_j_ref,
    gain_ref,
    shift_ref,
    qkvg_ref,
    out_w_ref,
    result_ref,
):
    width = H * DH
    mid = mid_ref[0].astype(F32)
    att = layer_norm(mid, gain_ref[...], shift_ref[...]).astype(BF16)
    heads = dot_nn(att, qkvg_ref[...])
    queries = (heads[:, :width] * DH ** (-0.5)).astype(BF16)
    keys = heads[:, width : 2 * width].astype(BF16)
    vals = heads[:, 2 * width : 3 * width].astype(BF16)
    gate = jax.nn.sigmoid(heads[:, 3 * width :])
    attended = []
    for head in range(H):
        lanes = slice(head * DH, (head + 1) * DH)
        scores = dot_nt(queries[:, lanes], keys[:, lanes]) + extra_ref[head]
        powers = jnp.exp(scores - jnp.max(scores, axis=1, keepdims=True))
        total = jnp.sum(powers, axis=1, keepdims=True)
        attended.append(dot_nn(powers.astype(BF16), vals[:, lanes]) / total)
    gated = (gate * jnp.concatenate(attended, axis=1)).astype(BF16)
    update = dot_nn(gated, out_w_ref[...])
    mask = valid_i_ref[...] * valid_j_ref[0]
    result_ref[0] = (mid + mask * update).astype(BF16)


def greet(peers):
    barrier = pltpu.get_barrier_semaphore()
    for peer in peers:
        pl.semaphore_signal(barrier, inc=1, device_id=peer, device_id_type=MESH)
    pl.semaphore_wait(barrier, len(peers))


def gather_kernel(nr, nq, src, out, own_sem, col_send, col_recv, row_send, row_recv):
    r, q = lax.axis_index("row"), lax.axis_index("col")
    row_peers = [(lax.rem(r + e, nr), q) for e in range(1, nr)]
    col_peers = [(r, lax.rem(q + d, nq)) for d in range(1, nq)]
    greet(row_peers + col_peers)
    own = pltpu.make_async_copy(src, out.at[q, r], own_sem)
    own.start()
    over_col = []
    for d in range(1, nq):
        over_col.append(
            pltpu.make_async_remote_copy(
                src_ref=src,
                dst_ref=out.at[q, r],
                send_sem=col_send.at[d - 1],
                recv_sem=col_recv.at[d - 1],
                device_id=col_peers[d - 1],
                device_id_type=MESH,
            )
        )
        over_col[-1].start()
    over_row = []
    for d in range(nq):
        source = lax.rem(q + nq - d, nq)
        block = src if d == 0 else out.at[source, r]
        if d > 0:
            over_col[d - 1].wait_recv()
        for e in range(1, nr):
            over_row.append(
                pltpu.make_async_remote_copy(
                    src_ref=block,
                    dst_ref=out.at[source, r],
                    send_sem=row_send.at[e - 1, d],
                    recv_sem=row_recv.at[e - 1, d],
                    device_id=row_peers[e - 1],
                    device_id_type=MESH,
                )
            )
            over_row[-1].start()
    own.wait()
    for copy in over_row:
        copy.wait_recv()
    for copy in over_col + over_row:
        copy.wait_send()


def gather_all(block, nr, nq):
    return pl.pallas_call(
        functools.partial(gather_kernel, nr, nq),
        out_shape=jax.ShapeDtypeStruct((nq, nr) + block.shape, block.dtype),
        in_specs=[pl.BlockSpec(memory_space=pltpu.VMEM)],
        out_specs=pl.BlockSpec(memory_space=pltpu.VMEM),
        scratch_shapes=[
            pltpu.SemaphoreType.DMA,
            pltpu.SemaphoreType.DMA((nq - 1,)),
            pltpu.SemaphoreType.DMA((nq - 1,)),
            pltpu.SemaphoreType.DMA((nr - 1, nq)),
            pltpu.SemaphoreType.DMA((nr - 1, nq)),
        ],
        compiler_params=pltpu.CompilerParams(
            collective_id=0, has_side_effects=True, vmem_limit_bytes=VMEM_LIMIT
        ),
    )(block)


def swap_kernel(nr, gathers_rows, src, out, own_sem, send, recv):
    r, q = lax.axis_index("row"), lax.axis_index("col")
    peers = [(lax.rem(r + e, nr), q) for e in range(1, nr)]
    greet(peers)

    def outgoing(partner):
        return src.at[partner] if gathers_rows else src.at[:, partner]

    landing = out.at[:, r] if gathers_rows else out.at[r]
    copies = []
    for e in range(1, nr):
        copies.append(
            pltpu.make_async_remote_copy(
                src_ref=outgoing(peers[e - 1][0]),
                dst_ref=landing,
                send_sem=send.at[e - 1],
                recv_sem=recv.at[e - 1],
                device_id=peers[e - 1],
                device_id_type=MESH,
            )
        )
        copies[-1].start()
    own = pltpu.make_async_copy(outgoing(r), landing, own_sem)
    own.start()
    own.wait()
    for copy in copies:
        copy.wait()


def swap_rows(array, nr, gathers_rows):
    shape = (array.shape[1], array.shape[0]) + array.shape[2:]
    return pl.pallas_call(
        functools.partial(swap_kernel, nr, gathers_rows),
        out_shape=jax.ShapeDtypeStruct(shape, array.dtype),
        in_specs=[pl.BlockSpec(memory_space=pltpu.VMEM)],
        out_specs=pl.BlockSpec(memory_space=pltpu.VMEM),
        scratch_shapes=[
            pltpu.SemaphoreType.DMA,
            pltpu.SemaphoreType.DMA((nr - 1,)),
            pltpu.SemaphoreType.DMA((nr - 1,)),
        ],
        compiler_params=pltpu.CompilerParams(
            collective_id=1 if gathers_rows else 2,
            has_side_effects=True,
            vmem_limit_bytes=VMEM_LIMIT,
        ),
    )(array)


def step_call(kernel, steps, ins, outs):
    def spec(shape, dim):
        block = tuple(n // steps if d == dim else n for d, n in enumerate(shape))
        return pl.BlockSpec(block, lambda c: tuple(c if d == dim else 0 for d in range(len(shape))))

    return pl.pallas_call(
        kernel,
        grid=(steps,),
        in_specs=[spec(a.shape, dim) for a, dim in ins],
        out_specs=[spec(shape, dim) for shape, _, dim in outs],
        out_shape=[jax.ShapeDtypeStruct(shape, t) for shape, t, _ in outs],
        compiler_params=pltpu.CompilerParams(vmem_limit_bytes=VMEM_LIMIT),
    )(*[a for a, _ in ins])


def on_device(
    pair,
    block_chain,
    block_valid,
    tri_norm_gain,
    tri_norm_bias,
    tri_in_weight,
    tri_gate_weight,
    out_norm_gain,
    out_norm_bias,
    tri_out_weight,
    att_norm_gain,
    att_norm_bias,
    qkvg_weight,
    bias_weight,
    inter_chain,
    att_out_weight,
):
    row_count, col_count, channels = pair.shape
    hidden = tri_out_weight.shape[0]
    row_devices = lax.axis_size("row")
    col_devices = lax.axis_size("col")
    devices = row_devices * col_devices
    residues = row_count * row_devices
    strip = col_count // row_devices
    axes = ("col", "row")
    residue_valid = jnp.repeat(block_valid, MB).astype(F32)
    residue_chain = jnp.repeat(block_chain, MB)
    strip_start = lax.axis_index("col") * col_count + lax.axis_index("row") * strip
    valid_j = lax.dynamic_slice_in_dim(residue_valid, strip_start, strip)[:, None]

    share = hidden // devices
    flat = strip * residues
    steps = strip // 2 if strip % 2 == 0 else 1
    by_column = jnp.swapaxes(pair, 0, 1).reshape(row_devices, strip, row_count, channels)
    own = swap_rows(by_column, row_devices, True).reshape(strip, residues, channels)
    in_t = (
        tri_in_weight.reshape(channels, 2, 2, devices, share)
        .transpose(2, 3, 1, 4, 0)
        .reshape(4 * hidden, channels)
    )
    mask = (valid_j * residue_valid[None, :]).reshape(1, flat)
    sides, tri_gate = step_call(
        project_kernel,
        steps,
        [
            (own, 0),
            (mask, 1),
            (tri_norm_gain[None, :], None),
            (tri_norm_bias[None, :], None),
            (in_t, None),
            (tri_gate_weight, None),
        ],
        [((2 * hidden, flat), BF16, 1), ((strip, residues, channels), F32, 0)],
    )
    spread = lax.all_to_all(
        sides.reshape(devices, 2 * share, flat), axes, split_axis=0, concat_axis=0, tiled=True
    ).reshape(devices, 2, share, strip, residues)
    product = jnp.einsum(
        "pcki,pckj->cji", spread[:, 0], spread[:, 1], preferred_element_type=F32
    ).astype(BF16)
    product = jnp.swapaxes(product.reshape(share, devices, flat), 0, 1)
    product = lax.all_to_all(product, axes, split_axis=0, concat_axis=0, tiled=True)
    mid, bias = step_call(
        middle_kernel,
        steps,
        [
            (own, 0),
            (product.reshape(hidden, flat), 1),
            (tri_gate, 0),
            (out_norm_gain[:, None], None),
            (out_norm_bias[:, None], None),
            (tri_out_weight, None),
            (att_norm_gain[None, :], None),
            (att_norm_bias[None, :], None),
            (bias_weight.T, None),
        ],
        [((strip, residues, channels), BF16, 0), ((H, flat), BF16, 1)],
    )
    bias = gather_all(bias, row_devices, col_devices).reshape(devices, H, strip, residues)
    bias = jnp.swapaxes(bias, 0, 1).reshape(H, residues, residues)
    crossing = (residue_chain[:, None] != residue_chain[None, :]).astype(F32)
    extra = (
        bias.astype(F32)
        + inter_chain[:, None, None] * crossing[None]
        + (MASK_NEG * (residue_valid - 1.0))[None, None, :]
    )
    (result,) = step_call(
        attention_kernel,
        strip,
        [
            (mid, 0),
            (extra, None),
            (residue_valid[:, None], None),
            (valid_j[:, :, None], 0),
            (att_norm_gain[None, :], None),
            (att_norm_bias[None, :], None),
            (qkvg_weight, None),
            (att_out_weight, None),
        ],
        [((strip, residues, channels), BF16, 0)],
    )
    result = swap_rows(
        result.reshape(strip, row_devices, row_count, channels), row_devices, False
    ).reshape(col_count, row_count, channels)
    return jnp.swapaxes(result, 0, 1)


def solution(mesh):
    placed = (P("row", "col", None),) + (P(),) * 15
    return jax.shard_map(
        on_device, mesh=mesh, in_specs=placed, out_specs=P("row", "col", None), check_vma=False
    )
```

time: 237 us -> 168 us (0.71)
  blocking collectives: 138 us -> 45.6 us
  Pallas kernels: 32.6 us -> 68.4 us
  waiting for transfers between devices: 32.5 us -> 19.2 us
  starting transfers between devices: 8.41 us -> 3.48 us
  local copies, waits for them, and re-layouts: 20.3 us -> 25.2 us
    all_gather x1 -> x0, blocking collectives: 71.7 us -> none  [on_device(): bias = lax.all_gather(bias, axes, axis=0, tiled=True)]
    pallas_call x3 -> x6, Pallas kernels: 32.6 us -> 68.4 us  [the longest x3 27.8 us: step_call(): pl.pallas_call(kernel, grid=(steps,), in_specs=[spec(a.shape, dim) for a,...]
    all_to_all x2 -> x1, blocking collectives: 66.4 us -> 45.6 us  [on_device(): lax.all_to_all(sides.reshape(devices, 2 * share, flat), axes, split_axis=...]
    all_to_all x2 -> x1, waiting for transfers between devices: 32.5 us -> 19.2 us  [on_device(): lax.all_to_all(product, axes, split_axis=0, concat_axis=0, tiled=True)]
    reshape x0 -> x5, local copies, waits for them, and re-layouts: none -> 11.5 us  [the longest x1 5.23 us: on_device(): spread = lax.all_to_all(sides.reshape(devices, 2 * share, flat), axes, sp...]
    all_to_all x2 -> x1, starting transfers between devices: 8.41 us -> 3.48 us  [on_device(): lax.all_to_all(product, axes, split_axis=0, concat_axis=0, tiled=True)]
    all_to_all x5 -> x0, local copies, waits for them, and re-layouts: 4.34 us -> none  [the longest x2 3.05 us: on_device(): lax.all_to_all(product, axes, split_axis=1, concat_axis=0, tiled=True)]
    convert_element_type x1 -> x2, local copies, waits for them, and re-layouts: 1.73 us -> 5.13 us  [on_device(): bias.astype(F32) + inter_chain[:, None, None] * crossing[None]]
  transfers between devices with their start and end apart: 2 -> 1, of which waited for: 2 -> 1; matrix products, arithmetic and copies ran while one was open for 2% -> 2% of each run, Pallas kernels for 0% -> 0%
where the time goes in v2:
time: 168 us; the launch traced here: 167 us
  Pallas kernels  68.4 us (41%)
  blocking collectives  45.6 us (27%)
  local copies, waits for them, and re-layouts  25.2 us (15%)
  waiting for transfers between devices  19.2 us (11%)
  starting transfers between devices  3.48 us (2%)
  matrix products  2.63 us (2%)
  other arithmetic  2.5 us (1%)
    all_to_all x1, blocking collectives, on_device(): lax.all_to_all(sides.reshape(devices, 2 * share, flat), axes, split_axis=...  45.6 us
    pallas_call x3, Pallas kernels, step_call(): pl.pallas_call(kernel, grid=(steps,), in_specs=[spec(a.shape, dim) for a,...  27.8 us
    pallas_call x2, Pallas kernels, swap_rows(): pl.pallas_call(functools.partial(swap_kernel, nr, gathers_rows), out_shap...  25 us
    all_to_all x1, waiting for transfers between devices, on_device(): lax.all_to_all(product, axes, split_axis=0, concat_axis=0, tiled=True)  19.2 us
    pallas_call x1, Pallas kernels, gather_all(): pl.pallas_call(functools.partial(gather_kernel, nr, nq), out_shape=jax.Sh...  15.6 us
    reshape x1, local copies, waits for them, and re-layouts, on_device(): spread = lax.all_to_all(sides.reshape(devices, 2 * share, flat), axes, sp...  5.23 us
    convert_element_type x2, local copies, waits for them, and re-layouts, on_device(): bias.astype(F32) + inter_chain[:, None, None] * crossing[None]  5.13 us
    reshape x2, local copies, waits for them, and re-layouts, on_device(): product = jnp.swapaxes(product.reshape(share, devices, flat), 0, 1)  3.61 us
  transfers between devices with their start and end apart: 1, of which 1 were waited for; matrix products, arithmetic and copies ran while one was open for 2% of the time, Pallas kernels for 0%

profile of v2, /device:TPU:0, one launch (start us, length us, event | category | flops | bytes accessed | tf_op | source)
XLA Modules:
  0.0 167.4 jit_solution(3835974279942037102)
XLA Ops:
  1.1 1.3 copy.25
  2.4 13.8 %shard_map.154 = bf16[10,4,80,128]{3,2,1,0:T(8,128)(2,1)S(1)} custom-call(bf16[4,10,80,128]{3,2,1,0:T(8,128)(2,1)S(1)} %bitcast.40), custom_call_target="tpu_custom_call" | custom-call | tf_op jit(solution)/shard_map/pallas_call | solution.py:211
  16.4 3.1 %shard_map.155 = (bf16[256,3200]{1,0:T(8,128)(2,1)S(1)}, f32[10,320,128]{2,1,0:T(8,128)S(1)}) custom-call(bf16[10,320,128]{2,1,0:T(8,128)(2,1)S(1)} %bitcast.36, f32[1,3200]{1,0:T(1,128)S(1)} %mul.57.mask_ref, f32[1,128]{1,0:T(1,128)S(1)} %bitcast.48, f32[1,128]{1,0:T(1,128)S(1)} %bitcast.49, bf16[512,128]{1,0:T(8,128)(2,1)S(1)} %bitcast.42, ...), custom_call_target="tpu_custom_call" | custom-call | tf_op jit(solution)/shard_map/pallas_call | solution.py:234
  19.5 45.6 %all_to_all.10 = bf16[32,8,3200]{2,1,0:T(8,128)(2,1)} all-to-all(bf16[32,8,3200]{2,1,0:T(8,128)(2,1)S(1)} %bitcast.41), channel_id=1, replica_groups=mesh['row'=4,'col'=8] {'col','row'}, dimensions={0} | all-to-all | bytes 3276800 | tf_op jit(solution)/shard_map/all_to_all | solution.py:299
  65.1 5.2 %reshape.125 = bf16[32,2,4,10,320]{4,3,2,1,0:T(8,128)(2,1)} reshape(bf16[32,8,3200]{2,1,0:T(8,128)(2,1)} %all_to_all.10) | data formatting | bytes 3276800 | tf_op jit(solution)/shard_map/reshape | solution.py:301
  70.4 2.2 %fusion.1 = (bf16[32,1,4,10,320]{4,3,2,1,0:T(8,128)(2,1)S(1)}, bf16[32,1,4,10,320]{4,3,2,1,0:T(8,128)(2,1)S(1)}) fusion(bf16[32,2,4,10,320]{4,3,2,1,0:T(8,128)(2,1)} %reshape.125), kind=kLoop, calls=%fused_computation.10 | loop fusion | bytes 3276800 | tf_op jit(solution)/shard_map/slice | solution.py:303
  72.6 2.6 %bitcast_convert_fusion = bf16[4,320,320]{2,1,0:T(8,128)(2,1)} fusion(bf16[32,1,4,10,320]{4,3,2,1,0:T(8,128)(2,1)S(1)} %get-tuple-element.14, bf16[32,1,4,10,320]{4,3,2,1,0:T(8,128)(2,1)S(1)} %get-tuple-element.13), kind=kOutput, calls=%fused_computation | convolution fusion | flops 262553600 | bytes 2457600 | tf_op jit(solution)/shard_map/pcki,pckj->cji/dot_general | solution.py:302
  75.2 2.3 %reshape.126 = bf16[4,32,3200]{2,1,0:T(8,128)(2,1)S(1)} reshape(bf16[4,320,320]{2,1,0:T(8,128)(2,1)} %bitcast_convert_fusion) | data formatting | bytes 1638400 | tf_op jit(solution)/shard_map/reshape | solution.py:305
  77.6 1.3 copy.51
  78.9 3.5 %all-to-all-start.1 = ((bf16[32,4,3200]{2,1,0:T(4,128)(2,1)}), bf16[32,4,3200]{2,1,0:T(4,128)(2,1)}, u32[]{:S(2)}, u32[]{:S(2)}) async-start(bf16[32,4,3200]{2,1,0:T(4,128)(2,1)} %bitcast.52), calls=%async_computation.1 | async-start | bytes 1638400 | tf_op jit(solution)/shard_map/all_to_all | solution.py:306
  82.7 0.7 copy.32.out_shift_ref
  84.3 0.9 compare_convert_fusion
  85.2 19.2 %all-to-all-done.1 = bf16[32,4,3200]{2,1,0:T(4,128)(2,1)} async-done(((bf16[32,4,3200]{2,1,0:T(4,128)(2,1)}), bf16[32,4,3200]{2,1,0:T(4,128)(2,1)}, u32[]{:S(2)}, u32[]{:S(2)}) %all-to-all-start.1) | async-done | bytes 819232 | tf_op jit(solution)/shard_map/all_to_all | solution.py:306
  104.4 1.6 reshape.127.product_ref
  106.0 0.8 copy-done.2
  107.5 3.4 %shard_map.156 = (bf16[10,320,128]{2,1,0:T(8,128)(2,1)S(1)}, bf16[4,3200]{1,0:T(4,128)(2,1)S(1)}) custom-call(bf16[10,320,128]{2,1,0:T(8,128)(2,1)S(1)} %bitcast.37, bf16[128,3200]{1,0:T(8,128)(2,1)S(1)} %reshape.127.product_ref, f32[10,320,128]{2,1,0:T(8,128)S(1)} %get-tuple-element.10.gate_ref, f32[128,1]{1,0:T(8,128)S(1)} %copy.31.out_gain_ref, ...), custom_call_target="tpu_custom_call" | custom-call | tf_op jit(solution)/shard_map/pallas_call | solution.py:234
  110.9 0.9 copy-done
  111.8 15.6 %shard_map.157 = bf16[8,4,4,3200]{3,2,1,0:T(4,128)(2,1)S(1)} custom-call(bf16[4,3200]{1,0:T(4,128)(2,1)S(1)} %get-tuple-element.12.src), custom_call_target="tpu_custom_call" | custom-call | tf_op jit(solution)/shard_map/pallas_call | solution.py:162
  127.5 2.4 %reshape.131 = f32[32,4,10,320]{3,2,1,0:T(8,128)} reshape(bf16[8,4,4,3200]{3,2,1,0:T(4,128)(2,1)S(1)} %shard_map.157) | data formatting | bytes 2457600 | tf_op jit(solution)/shard_map/convert_element_type | solution.py:327
  129.9 2.7 %copy.33 = f32[4,32,10,320]{3,0,2,1:T(4,128)S(1)} copy(f32[4,32,10,320]{3,2,0,1:T(8,128)} %bitcast.50) | data formatting | bytes 3276800 | tf_op jit(solution)/shard_map/convert_element_type | solution.py:327
  132.9 0.8 copy-done.1
  133.8 21.3 %shard_map.158 = bf16[10,320,128]{2,1,0:T(8,128)(2,1)S(1)} custom-call(bf16[10,320,128]{2,1,0:T(8,128)(2,1)S(1)} %copy-done.1, f32[4,320,320]{2,1,0:T(8,128)S(1)} %fusion.extra_ref, f32[320,1]{1,0:T(8,128)S(1)} %convert_element_type.60.valid_i_ref, f32[10,1,1]{2,1,0:T(1,128)S(1)} %copy.36.valid_j_ref, f32[1,128]{1,0:T(1,128)S(1)} %bitcast.44, ...), custom_call_target="tpu_custom_call" | custom-call | tf_op jit(solution)/shard_map/pallas_call | solution.py:234
  155.1 11.2 %shard_map.159 = bf16[4,10,80,128]{3,2,1,0:T(8,128)(2,1)S(1)} custom-call(bf16[10,4,80,128]{3,2,1,0:T(8,128)(2,1)S(1)} %bitcast.38), custom_call_target="tpu_custom_call" | custom-call | tf_op jit(solution)/shard_map/pallas_call | solution.py:211
  166.3 1.1 copy.50
  (51 shorter events, 3.4 us)
Async XLA Ops:
  0.0 16.2 %copy-start.13 = (bf16[128,512]{1,0:T(8,128)(2,1)S(1)}, bf16[128,512]{1,0:T(8,128)(2,1)}, u32[]{:S(2)}) copy-start(bf16[128,512]{1,0:T(8,128)(2,1)} %param.21) | copy-start | bytes 393220
  0.0 16.4 %copy-start.10 = (f32[128]{0:T(128)S(1)}, f32[128]{0:T(128)}, u32[]{:S(2)}) copy-start(f32[128]{0:T(128)} %param.19) | copy-start | bytes 1540
  0.0 16.4 %copy-start.11 = (f32[128]{0:T(128)S(1)}, f32[128]{0:T(128)}, u32[]{:S(2)}) copy-start(f32[128]{0:T(128)} %param.20) | copy-start | bytes 1540
  0.0 16.4 %copy-start.6 = (bf16[128,128]{1,0:T(8,128)(2,1)S(1)}, bf16[128,128]{1,0:T(8,128)(2,1)}, u32[]{:S(2)}) copy-start(bf16[128,128]{1,0:T(8,128)(2,1)} %gate_w_ref.1) | copy-start | bytes 98308
  77.5 5.0 %copy-start.15 = (f32[128]{0:T(128)S(1)}, f32[128]{0:T(128)}, u32[]{:S(2)}) copy-start(f32[128]{0:T(128)} %param.23) | copy-start | bytes 1540
  77.5 5.1 %copy-start.16 = (f32[128]{0:T(128)S(1)}, f32[128]{0:T(128)}, u32[]{:S(2)}) copy-start(f32[128]{0:T(128)} %param.24) | copy-start | bytes 1540
  77.6 5.8 %copy-start.18 = (s32[5]{0:T(128)S(1)}, s32[5]{0:T(128)}, u32[]{:S(2)}) copy-start(s32[5]{0:T(128)} %param.17) | copy-start | bytes 64
  78.9 27.1 %copy-start.4 = (bf16[128,128]{1,0:T(8,128)(2,1)S(1)}, bf16[128,128]{1,0:T(8,128)(2,1)}, u32[]{:S(2)}) copy-start(bf16[128,128]{1,0:T(8,128)(2,1)} %out_w_ref.2) | copy-start | bytes 98308
  78.9 27.1 %copy-start.7 = (f32[128]{0:T(128)S(1)}, f32[128]{0:T(128)}, u32[]{:S(2)}) copy-start(f32[128]{0:T(128)} %param.26) | copy-start | bytes 1540
  78.9 27.1 %copy-start.8 = (f32[128]{0:T(128)S(1)}, f32[128]{0:T(128)}, u32[]{:S(2)}) copy-start(f32[128]{0:T(128)} %param.27) | copy-start | bytes 1540
  78.9 25.5 %all-to-all-start.1 = ((bf16[32,4,3200]{2,1,0:T(4,128)(2,1)}), bf16[32,4,3200]{2,1,0:T(4,128)(2,1)}, u32[]{:S(2)}, u32[]{:S(2)}) async-start(bf16[32,4,3200]{2,1,0:T(4,128)(2,1)} %bitcast.52), calls=%async_computation.1 | async-start | bytes 1638400 | tf_op jit(solution)/shard_map/all_to_all | solution.py:306
  106.0 0.8 copy-start.2
  106.9 0.7 copy-start.9
  110.9 0.9 copy-start
  129.9 2.7 %copy-start.12 = (f32[320,320]{1,0:T(8,128)S(1)}, f32[320,320]{1,0:T(8,128)}, u32[]{:S(2)}) copy-start(f32[320,320]{1,0:T(8,128)} %compare_convert_fusion) | copy-start | bytes 1228804
  129.9 2.7 %copy-start.14 = (f32[320]{0:T(512)S(1)}, f32[320]{0:T(512)}, u32[]{:S(2)}) copy-start(f32[320]{0:T(512)} %add_multiply_fusion) | copy-start | bytes 3844
  129.9 2.8 %copy-start.17 = (f32[4]{0:T(128)S(1)}, f32[4]{0:T(128)}, u32[]{:S(2)}) copy-start(f32[4]{0:T(128)} %param.30) | copy-start | bytes 52
  132.6 1.1 copy-start.1
  132.6 1.1 copy-start.3
  132.6 1.1 copy-start.5

commit v3 on v2

--- a/solution.py
+++ b/solution.py
@@ -13,6 +13,7 @@
 
 MASK_NEG = 10000.0
 EPS = 1e-05
+FILLED = -1e30
 F32 = jnp.float32
 BF16 = jnp.bfloat16
 MESH = pl.DeviceIdType.MESH
@@ -38,13 +39,19 @@
     return lax.dot_general(left, right, (((1,), (0,)), ((), ())), preferred_element_type=F32)
 
 
-def project_kernel(pair_ref, mask_ref, gain_ref, shift_ref, in_t_ref, gate_w_ref, sides_ref, gate_ref):
+def project_kernel(pair_ref, mask_ref, gain_ref, shift_ref, in_t_ref, sides_ref):
     columns, rows, channels = pair_ref.shape
     flat = pair_ref[...].reshape(columns * rows, channels).astype(F32)
     normed = layer_norm(flat, gain_ref[...], shift_ref[...]).astype(BF16)
     proj = dot_nt(in_t_ref[...], normed)
     half = sides_ref.shape[0]
     sides_ref[...] = (mask_ref[...] * jax.nn.sigmoid(proj[:half]) * proj[half:]).astype(BF16)
+
+
+def gate_kernel(pair_ref, gain_ref, shift_ref, gate_w_ref, gate_ref):
+    columns, rows, channels = pair_ref.shape
+    flat = pair_ref[...].reshape(columns * rows, channels).astype(F32)
+    normed = layer_norm(flat, gain_ref[...], shift_ref[...]).astype(BF16)
     gate = jax.nn.sigmoid(dot_nn(normed, gate_w_ref[...]))
     gate_ref[...] = gate.reshape(columns, rows, channels)
 
@@ -71,7 +78,13 @@
     mid = (flat + gate_ref[...].reshape(columns * rows, channels) * update).astype(BF16)
     mid_ref[...] = mid.reshape(columns, rows, channels)
     att = layer_norm(mid.astype(F32), att_gain_ref[...], att_shift_ref[...]).astype(BF16)
-    bias_ref[...] = dot_nt(bias_t_ref[...], att).astype(BF16)
+    bias = dot_nt(bias_t_ref[...], att).astype(BF16)
+    for column in range(columns):
+        bias_ref[column] = bias[:, column * rows : (column + 1) * rows]
+
+
+def stack_rows(parts):
+    return jnp.concatenate([part for part in parts if part.shape[0]], axis=0)
 
 
 def attention_kernel(
@@ -93,14 +106,25 @@
     keys = heads[:, width : 2 * width].astype(BF16)
     vals = heads[:, 2 * width : 3 * width].astype(BF16)
     gate = jax.nn.sigmoid(heads[:, 3 * width :])
-    attended = []
+    rows, padded = extra_ref.shape[1:]
+    lane_head = lax.broadcasted_iota(jnp.int32, (rows, width), 1) // DH
+    filler = jnp.zeros((padded - rows, width), BF16)
+    key_rows, val_rows, one_rows = [], [], []
     for head in range(H):
-        lanes = slice(head * DH, (head + 1) * DH)
-        scores = dot_nt(queries[:, lanes], keys[:, lanes]) + extra_ref[head]
-        powers = jnp.exp(scores - jnp.max(scores, axis=1, keepdims=True))
-        total = jnp.sum(powers, axis=1, keepdims=True)
-        attended.append(dot_nn(powers.astype(BF16), vals[:, lanes]) / total)
-    gated = (gate * jnp.concatenate(attended, axis=1)).astype(BF16)
+        inside = (lane_head == head).astype(F32).astype(BF16)
+        key_rows += [keys * inside, filler]
+        val_rows += [vals * inside, filler]
+        one_rows += [inside, filler]
+    scores = dot_nt(queries, stack_rows(key_rows))
+    powers = []
+    for head in range(H):
+        part = scores[:, head * padded : (head + 1) * padded] + extra_ref[head]
+        powers.append(jnp.exp(part - jnp.max(part, axis=1, keepdims=True)).astype(BF16))
+    sums = dot_nn(
+        jnp.concatenate(powers, axis=1),
+        jnp.concatenate([stack_rows(val_rows), stack_rows(one_rows)], axis=1),
+    )
+    gated = (gate * sums[:, :width] / sums[:, width:]).astype(BF16)
     update = dot_nn(gated, out_w_ref[...])
     mask = valid_i_ref[...] * valid_j_ref[0]
     result_ref[0] = (mid + mask * update).astype(BF16)
@@ -177,21 +201,16 @@
     )(block)
 
 
-def swap_kernel(nr, gathers_rows, src, out, own_sem, send, recv):
+def swap_kernel(nr, src, out, own_sem, send, recv):
     r, q = lax.axis_index("row"), lax.axis_index("col")
     peers = [(lax.rem(r + e, nr), q) for e in range(1, nr)]
     greet(peers)
-
-    def outgoing(partner):
-        return src.at[partner] if gathers_rows else src.at[:, partner]
-
-    landing = out.at[:, r] if gathers_rows else out.at[r]
     copies = []
     for e in range(1, nr):
         copies.append(
             pltpu.make_async_remote_copy(
-                src_ref=outgoing(peers[e - 1][0]),
-                dst_ref=landing,
+                src_ref=src.at[:, peers[e - 1][0]],
+                dst_ref=out.at[r],
                 send_sem=send.at[e - 1],
                 recv_sem=recv.at[e - 1],
                 device_id=peers[e - 1],
@@ -199,17 +218,17 @@
             )
         )
         copies[-1].start()
-    own = pltpu.make_async_copy(outgoing(r), landing, own_sem)
+    own = pltpu.make_async_copy(src.at[:, r], out.at[r], own_sem)
     own.start()
     own.wait()
     for copy in copies:
         copy.wait()
 
 
-def swap_rows(array, nr, gathers_rows):
+def swap_rows(array, nr):
     shape = (array.shape[1], array.shape[0]) + array.shape[2:]
     return pl.pallas_call(
-        functools.partial(swap_kernel, nr, gathers_rows),
+        functools.partial(swap_kernel, nr),
         out_shape=jax.ShapeDtypeStruct(shape, array.dtype),
         in_specs=[pl.BlockSpec(memory_space=pltpu.VMEM)],
         out_specs=pl.BlockSpec(memory_space=pltpu.VMEM),
@@ -219,11 +238,77 @@
             pltpu.SemaphoreType.DMA((nr - 1,)),
         ],
         compiler_params=pltpu.CompilerParams(
-            collective_id=1 if gathers_rows else 2,
-            has_side_effects=True,
-            vmem_limit_bytes=VMEM_LIMIT,
+            collective_id=2, has_side_effects=True, vmem_limit_bytes=VMEM_LIMIT
         ),
     )(array)
+
+
+def spread_kernel(nr, nq, sides, pair, spread, strip, own_sem, send, recv, row_send, row_recv):
+    r, q = lax.axis_index("row"), lax.axis_index("col")
+    devices = nr * nq
+    me = q * nr + r
+    others = [lax.rem(me + d, devices) for d in range(1, devices)]
+    places = [(lax.rem(other, nr), other // nr) for other in others]
+    greet(places)
+    copies = []
+    for d in range(devices - 1):
+        copies.append(
+            pltpu.make_async_remote_copy(
+                src_ref=sides.at[others[d]],
+                dst_ref=spread.at[me],
+                send_sem=send.at[d],
+                recv_sem=recv.at[d],
+                device_id=places[d],
+                device_id_type=MESH,
+            )
+        )
+        copies[-1].start()
+    for e in range(1, nr):
+        partner = lax.rem(r + e, nr)
+        copies.append(
+            pltpu.make_async_remote_copy(
+                src_ref=pair.at[partner],
+                dst_ref=strip.at[:, r],
+                send_sem=row_send.at[e - 1],
+                recv_sem=row_recv.at[e - 1],
+                device_id=(partner, q),
+                device_id_type=MESH,
+            )
+        )
+        copies[-1].start()
+    own = [
+        pltpu.make_async_copy(sides.at[me], spread.at[me], own_sem.at[0]),
+        pltpu.make_async_copy(pair.at[r], strip.at[:, r], own_sem.at[1]),
+    ]
+    for copy in own:
+        copy.start()
+    for copy in own:
+        copy.wait()
+    for copy in copies:
+        copy.wait()
+
+
+def spread_all(sides, pair, nr, nq):
+    shape = (pair.shape[1], pair.shape[0]) + pair.shape[2:]
+    return pl.pallas_call(
+        functools.partial(spread_kernel, nr, nq),
+        out_shape=[
+            jax.ShapeDtypeStruct(sides.shape, sides.dtype),
+            jax.ShapeDtypeStruct(shape, pair.dtype),
+        ],
+        in_specs=[pl.BlockSpec(memory_space=pltpu.VMEM)] * 2,
+        out_specs=[pl.BlockSpec(memory_space=pltpu.VMEM)] * 2,
+        scratch_shapes=[
+            pltpu.SemaphoreType.DMA((2,)),
+            pltpu.SemaphoreType.DMA((nr * nq - 1,)),
+            pltpu.SemaphoreType.DMA((nr * nq - 1,)),
+            pltpu.SemaphoreType.DMA((nr - 1,)),
+            pltpu.SemaphoreType.DMA((nr - 1,)),
+        ],
+        compiler_params=pltpu.CompilerParams(
+            collective_id=1, has_side_effects=True, vmem_limit_bytes=VMEM_LIMIT
+        ),
+    )(sides, pair)
 
 
 def step_call(kernel, steps, ins, outs):
@@ -275,32 +360,56 @@
     share = hidden // devices
     flat = strip * residues
     steps = strip // 2 if strip % 2 == 0 else 1
-    by_column = jnp.swapaxes(pair, 0, 1).reshape(row_devices, strip, row_count, channels)
-    own = swap_rows(by_column, row_devices, True).reshape(strip, residues, channels)
+    by_column = jnp.swapaxes(pair, 0, 1)
     in_t = (
         tri_in_weight.reshape(channels, 2, 2, devices, share)
         .transpose(2, 3, 1, 4, 0)
         .reshape(4 * hidden, channels)
     )
-    mask = (valid_j * residue_valid[None, :]).reshape(1, flat)
-    sides, tri_gate = step_call(
+    valid_rows = lax.dynamic_slice_in_dim(
+        residue_valid, lax.axis_index("row") * row_count, row_count
+    )
+    valid_cols = lax.dynamic_slice_in_dim(
+        residue_valid, lax.axis_index("col") * col_count, col_count
+    )
+    mask = (valid_cols[:, None] * valid_rows[None, :]).reshape(1, flat)
+    (sides,) = step_call(
         project_kernel,
         steps,
         [
-            (own, 0),
+            (by_column, 0),
             (mask, 1),
             (tri_norm_gain[None, :], None),
             (tri_norm_bias[None, :], None),
             (in_t, None),
+        ],
+        [((2 * hidden, flat), BF16, 1)],
+    )
+    spread, own = spread_all(
+        sides.reshape(devices, 2 * share, flat),
+        by_column.reshape(row_devices, strip, row_count, channels),
+        row_devices,
+        col_devices,
+    )
+    own = own.reshape(strip, residues, channels)
+    (tri_gate,) = step_call(
+        gate_kernel,
+        steps,
+        [
+            (own, 0),
+            (tri_norm_gain[None, :], None),
+            (tri_norm_bias[None, :], None),
             (tri_gate_weight, None),
         ],
-        [((2 * hidden, flat), BF16, 1), ((strip, residues, channels), F32, 0)],
-    )
-    spread = lax.all_to_all(
-        sides.reshape(devices, 2 * share, flat), axes, split_axis=0, concat_axis=0, tiled=True
-    ).reshape(devices, 2, share, strip, residues)
+        [((strip, residues, channels), F32, 0)],
+    )
+    spread = (
+        spread.reshape(col_devices, row_devices, 2, share, col_count, row_count)
+        .transpose(2, 3, 0, 4, 1, 5)
+        .reshape(2, share, residues, residues)
+    )
     product = jnp.einsum(
-        "pcki,pckj->cji", spread[:, 0], spread[:, 1], preferred_element_type=F32
+        "cki,ckj->cji", spread[0], spread[1], preferred_element_type=F32
     ).astype(BF16)
     product = jnp.swapaxes(product.reshape(share, devices, flat), 0, 1)
     product = lax.all_to_all(product, axes, split_axis=0, concat_axis=0, tiled=True)
@@ -318,16 +427,16 @@
             (att_norm_bias[None, :], None),
             (bias_weight.T, None),
         ],
-        [((strip, residues, channels), BF16, 0), ((H, flat), BF16, 1)],
-    )
-    bias = gather_all(bias, row_devices, col_devices).reshape(devices, H, strip, residues)
-    bias = jnp.swapaxes(bias, 0, 1).reshape(H, residues, residues)
+        [((strip, residues, channels), BF16, 0), ((strip, H, residues), BF16, 0)],
+    )
+    bias = gather_all(bias, row_devices, col_devices).reshape(residues, H, residues)
     crossing = (residue_chain[:, None] != residue_chain[None, :]).astype(F32)
     extra = (
-        bias.astype(F32)
+        jnp.swapaxes(bias, 0, 1).astype(F32)
         + inter_chain[:, None, None] * crossing[None]
         + (MASK_NEG * (residue_valid - 1.0))[None, None, :]
     )
+    extra = jnp.pad(extra, ((0, 0), (0, 0), (0, -residues % 128)), constant_values=FILLED)
     (result,) = step_call(
         attention_kernel,
         strip,
@@ -344,7 +453,7 @@
         [((strip, residues, channels), BF16, 0)],
     )
     result = swap_rows(
-        result.reshape(strip, row_devices, row_count, channels), row_devices, False
+        result.reshape(strip, row_devices, row_count, channels), row_devices
     ).reshape(col_count, row_count, channels)
     return jnp.swapaxes(result, 0, 1)
 

time: 168 us -> 149 us (0.89)
  blocking collectives: 45.6 us -> 0 us
  Pallas kernels: 68.4 us -> 89.4 us
  starting transfers between devices: 3.48 us -> 12 us
  waiting for transfers between devices: 19.2 us -> 16.9 us
    all_to_all x1 -> x0, blocking collectives: 45.6 us -> none  [on_device(): lax.all_to_all(sides.reshape(devices, 2 * share, flat), axes, split_axis=...]
    pallas_call x2, Pallas kernels: 25 us -> 48.2 us  [the longest x1 37 us: spread_all(): pl.pallas_call(functools.partial(spread_kernel, nr, nq), out_shape=[jax.S...]
    all_to_all x1, starting transfers between devices: 3.48 us -> 12 us  [on_device(): lax.all_to_all(product, axes, split_axis=0, concat_axis=0, tiled=True)]
    convert_element_type x2 -> x0, local copies, waits for them, and re-layouts: 5.13 us -> none  [on_device(): bias.astype(F32) + inter_chain[:, None, None] * crossing[None]]
    pallas_call x3 -> x4, Pallas kernels: 27.8 us -> 24 us  [step_call(): pl.pallas_call(kernel, grid=(steps,), in_specs=[spec(a.shape, dim) for a,...]
    reshape x1 -> x2, local copies, waits for them, and re-layouts: 5.23 us -> 8.97 us  [on_device(): spread.reshape(col_devices, row_devices, 2, share, col_count, row_count)]
    squeeze x0 -> x2, local copies, waits for them, and re-layouts: none -> 3.37 us  [the longest x1 1.69 us: on_device(): spread[0]]
    all_to_all x1, waiting for transfers between devices: 19.2 us -> 16.9 us  [on_device(): lax.all_to_all(product, axes, split_axis=0, concat_axis=0, tiled=True)]
  transfers between devices with their start and end apart: 1 -> 1, of which waited for: 1 -> 1; matrix products, arithmetic and copies ran while one was open for 2% -> 2% of each run, Pallas kernels for 0% -> 1%
where the time goes in v3:
time: 149 us
  Pallas kernels  89.4 us (60%)
  local copies, waits for them, and re-layouts  25 us (17%)
  waiting for transfers between devices  16.9 us (11%)
  starting transfers between devices  12 us (8%)
  other arithmetic  2.89 us (2%)
  matrix products  2.01 us (1%)
    pallas_call x1, Pallas kernels, spread_all(): pl.pallas_call(functools.partial(spread_kernel, nr, nq), out_shape=[jax.S...  37 us
    pallas_call x4, Pallas kernels, step_call(): pl.pallas_call(kernel, grid=(steps,), in_specs=[spec(a.shape, dim) for a,...  24 us
    pallas_call x1, Pallas kernels, gather_all(): pl.pallas_call(functools.partial(gather_kernel, nr, nq), out_shape=jax.Sh...  17.3 us
    all_to_all x1, waiting for transfers between devices, on_device(): lax.all_to_all(product, axes, split_axis=0, concat_axis=0, tiled=True)  16.9 us
    all_to_all x1, starting transfers between devices, on_device(): lax.all_to_all(product, axes, split_axis=0, concat_axis=0, tiled=True)  12 us
    pallas_call x1, Pallas kernels, swap_rows(): pl.pallas_call(functools.partial(swap_kernel, nr), out_shape=jax.ShapeDty...  11.1 us
    reshape x2, local copies, waits for them, and re-layouts, on_device(): spread.reshape(col_devices, row_devices, 2, share, col_count, row_count)  8.97 us
    unnamed x44, local copies, waits for them, and re-layouts  4.65 us
  transfers between devices with their start and end apart: 1, of which 1 were waited for; matrix products, arithmetic and copies ran while one was open for 2% of the time, Pallas kernels for 1%

profile of v3, /device:TPU:0, one launch (start us, length us, event | category | flops | bytes accessed | tf_op | source)
XLA Modules:
  0.0 148.6 jit_solution(15068000277382950063)
XLA Ops:
  0.0 1.3 copy.49
  2.4 1.0 copy.28
  3.5 3.1 %shard_map.154 = bf16[256,3200]{1,0:T(8,128)(2,1)S(1)} custom-call(bf16[40,80,128]{2,1,0:T(8,128)(2,1)S(1)} %bitcast.39, f32[1,3200]{1,0:T(1,128)S(1)} %mul.61.mask_ref, f32[1,128]{1,0:T(1,128)S(1)} %bitcast.51, f32[1,128]{1,0:T(1,128)S(1)} %bitcast.53, bf16[512,128]{1,0:T(8,128)(2,1)S(1)} %bitcast.46), custom_call_target="tpu_custom_call" | custom-call | tf_op jit(solution)/shard_map/pallas_call | solution.py:319
  6.6 37.0 %shard_map.155 = (bf16[32,8,3200]{2,1,0:T(8,128)(2,1)S(1)}, bf16[10,4,80,128]{3,2,1,0:T(8,128)(2,1)S(1)}) custom-call(bf16[32,8,3200]{2,1,0:T(8,128)(2,1)S(1)} %bitcast.41, bf16[4,10,80,128]{3,2,1,0:T(8,128)(2,1)S(1)} %bitcast.40), custom_call_target="tpu_custom_call" | custom-call | tf_op jit(solution)/shard_map/pallas_call | solution.py:293
  43.7 3.9 %reshape.123 = bf16[8,4,2,4,40,80]{5,4,3,2,1,0:T(8,128)(2,1)} reshape(bf16[32,8,3200]{2,1,0:T(8,128)(2,1)S(1)} %get-tuple-element.10) | data formatting | bytes 3276800 | tf_op jit(solution)/shard_map/reshape | solution.py:407
  47.5 5.1 %copy.46 = bf16[8,4,2,4,40,80]{5,1,4,0,3,2:T(4,128)(2,1)S(1)} copy(bf16[8,4,2,4,40,80]{5,4,3,2,1,0:T(8,128)(2,1)} %reshape.123) | data formatting | bytes 3276800 | tf_op jit(solution)/shard_map/reshape | solution.py:407
  52.6 0.9 fusion.1
  53.6 1.7 %squeeze.6 = bf16[4,320,320]{2,1,0:T(8,128)(2,1)} reshape(bf16[1,4,8,40,4,80]{5,4,3,2,1,0:T(4,128)(2,1)S(1)} %get-tuple-element.14) | data formatting | bytes 1638400 | tf_op jit(solution)/shard_map/squeeze | solution.py:412
  55.3 1.7 %squeeze.7 = bf16[4,320,320]{2,1,0:T(8,128)(2,1)} reshape(bf16[1,4,8,40,4,80]{5,4,3,2,1,0:T(4,128)(2,1)S(1)} %get-tuple-element.13) | data formatting | bytes 1638400 | tf_op jit(solution)/shard_map/squeeze | solution.py:412
  57.0 2.0 %convolution_convert_fusion = bf16[4,320,320]{2,1,0:T(8,128)(2,1)S(1)} fusion(bf16[4,320,320]{2,1,0:T(8,128)(2,1)S(1)} %copy-done.12, bf16[4,320,320]{2,1,0:T(8,128)(2,1)} %squeeze.7), kind=kOutput, calls=%fused_computation.3 | convolution fusion | flops 262553600 | bytes 2457600 | tf_op jit(solution)/shard_map/cki,ckj->cji/dot_general | solution.py:411
  59.0 1.1 reshape.124
  60.2 1.3 copy.48
  61.5 12.0 %all-to-all-start = ((bf16[32,4,3200]{2,1,0:T(4,128)(2,1)}), bf16[32,4,3200]{2,1,0:T(4,128)(2,1)}, u32[]{:S(2)}, u32[]{:S(2)}) async-start(bf16[32,4,3200]{2,1,0:T(4,128)(2,1)} %bitcast.38), calls=%async_computation | async-start | bytes 1638400 | tf_op jit(solution)/shard_map/all_to_all | solution.py:415
  75.0 2.0 %shard_map.156.gate_ref = f32[10,320,128]{2,1,0:T(8,128)S(1)} custom-call(bf16[10,320,128]{2,1,0:T(8,128)(2,1)S(1)} %bitcast.42, f32[1,128]{1,0:T(1,128)S(1)} %bitcast.52, f32[1,128]{1,0:T(1,128)S(1)} %bitcast.54, bf16[128,128]{1,0:T(8,128)(2,1)S(1)} %copy-done.2), custom_call_target="tpu_custom_call" | custom-call | tf_op jit(solution)/shard_map/pallas_call | solution.py:319
  77.6 0.9 compare_convert_fusion
  78.5 16.9 %all-to-all-done = bf16[32,4,3200]{2,1,0:T(4,128)(2,1)} async-done(((bf16[32,4,3200]{2,1,0:T(4,128)(2,1)}), bf16[32,4,3200]{2,1,0:T(4,128)(2,1)}, u32[]{:S(2)}, u32[]{:S(2)}) %all-to-all-start) | async-done | bytes 819232 | tf_op jit(solution)/shard_map/all_to_all | solution.py:415
  95.4 1.6 %reshape.125.product_ref = bf16[128,3200]{1,0:T(8,128)(2,1)S(1)} reshape(bf16[32,4,3200]{2,1,0:T(4,128)(2,1)} %all-to-all-done) | data formatting | bytes 1638400 | tf_op jit(solution)/shard_map/reshape | solution.py:421
  97.1 0.8 copy-done
  98.6 3.7 %shard_map.157 = (bf16[10,320,128]{2,1,0:T(8,128)(2,1)S(1)}, bf16[10,4,320]{2,1,0:T(4,128)(2,1)S(1)}) custom-call(bf16[10,320,128]{2,1,0:T(8,128)(2,1)S(1)} %bitcast.43, bf16[128,3200]{1,0:T(8,128)(2,1)S(1)} %reshape.125.product_ref, f32[10,320,128]{2,1,0:T(8,128)S(1)} %shard_map.156.gate_ref, f32[128,1]{1,0:T(8,128)S(1)} %copy.33.out_gain_ref, ...), custom_call_target="tpu_custom_call" | custom-call | tf_op jit(solution)/shard_map/pallas_call | solution.py:319
  102.3 17.3 %shard_map.158 = bf16[8,4,10,4,320]{4,3,2,1,0:T(4,128)(2,1)S(1)} custom-call(bf16[10,4,320]{2,1,0:T(4,128)(2,1)S(1)} %get-tuple-element.12.src), custom_call_target="tpu_custom_call" | custom-call | tf_op jit(solution)/shard_map/pallas_call | solution.py:186
  120.5 0.7 copy-done.1
  121.2 15.2 %shard_map.159 = bf16[10,320,128]{2,1,0:T(8,128)(2,1)S(1)} custom-call(bf16[10,320,128]{2,1,0:T(8,128)(2,1)S(1)} %get-tuple-element.11.mid_ref, f32[4,320,384]{2,1,0:T(8,128)S(1)} %pad.4.extra_ref, f32[320,1]{1,0:T(8,128)S(1)} %convert_element_type.51.valid_i_ref, f32[10,1,1]{2,1,0:T(1,128)S(1)} %copy.37.valid_j_ref, f32[1,128]{1,0:T(1,128)S(1)} %bitcast.48, ...), custom_call_target="tpu_custom_call" | custom-call | tf_op jit(solution)/shard_map/pallas_call | solution.py:319
  136.4 11.1 %shard_map.160 = bf16[4,10,80,128]{3,2,1,0:T(8,128)(2,1)S(1)} custom-call(bf16[10,4,80,128]{3,2,1,0:T(8,128)(2,1)S(1)} %bitcast.44), custom_call_target="tpu_custom_call" | custom-call | tf_op jit(solution)/shard_map/pallas_call | solution.py:230
  147.5 1.1 copy.47
  (59 shorter events, 4.6 us)
Async XLA Ops:
  0.0 3.5 %copy-start.7 = (f32[128]{0:T(128)S(1)}, f32[128]{0:T(128)}, u32[]{:S(2)}) copy-start(f32[128]{0:T(128)} %param.19) | copy-start | bytes 1540
  0.0 3.5 %copy-start.9 = (f32[128]{0:T(128)S(1)}, f32[128]{0:T(128)}, u32[]{:S(2)}) copy-start(f32[128]{0:T(128)} %param.20) | copy-start | bytes 1540
  2.1 72.7 %copy-start.15 = (f32[320]{0:T(512)}, f32[320]{0:T(512)S(1)}, u32[]{:S(2)}) copy-start(f32[320]{0:T(512)S(1)} %convert_element_type.42) | copy-start | bytes 3844
  55.3 1.7 %copy-start.12 = (bf16[4,320,320]{2,1,0:T(8,128)(2,1)S(1)}, bf16[4,320,320]{2,1,0:T(8,128)(2,1)}, u32[]{:S(2)}) copy-start(bf16[4,320,320]{2,1,0:T(8,128)(2,1)} %squeeze.6) | copy-start | bytes 2457604
  60.1 13.6 %copy-start.17 = (f32[128]{0:T(128)S(1)}, f32[128]{0:T(128)}, u32[]{:S(2)}) copy-start(f32[128]{0:T(128)} %param.23) | copy-start | bytes 1540
  60.2 13.7 %copy-start.18 = (f32[128]{0:T(128)S(1)}, f32[128]{0:T(128)}, u32[]{:S(2)}) copy-start(f32[128]{0:T(128)} %param.24) | copy-start | bytes 1540
  60.2 14.4 %copy-start.20 = (s32[5]{0:T(128)S(1)}, s32[5]{0:T(128)}, u32[]{:S(2)}) copy-start(s32[5]{0:T(128)} %param.17) | copy-start | bytes 64
  60.2 14.8 %copy-start.2 = (bf16[128,128]{1,0:T(8,128)(2,1)S(1)}, bf16[128,128]{1,0:T(8,128)(2,1)}, u32[]{:S(2)}) copy-start(bf16[128,128]{1,0:T(8,128)(2,1)} %gate_w_ref.1) | copy-start | bytes 98308
  60.2 14.7 %copy-start.8 = (f32[128]{0:T(128)S(1)}, f32[128]{0:T(128)}, u32[]{:S(2)}) copy-start(f32[128]{0:T(128)} %param.19) | copy-start | bytes 1540
  60.2 14.7 %copy-start.10 = (f32[128]{0:T(128)S(1)}, f32[128]{0:T(128)}, u32[]{:S(2)}) copy-start(f32[128]{0:T(128)} %param.20) | copy-start | bytes 1540
  61.5 33.9 %all-to-all-start = ((bf16[32,4,3200]{2,1,0:T(4,128)(2,1)}), bf16[32,4,3200]{2,1,0:T(4,128)(2,1)}, u32[]{:S(2)}, u32[]{:S(2)}) async-start(bf16[32,4,3200]{2,1,0:T(4,128)(2,1)} %bitcast.38), calls=%async_computation | async-start | bytes 1638400 | tf_op jit(solution)/shard_map/all_to_all | solution.py:415
  74.8 2.1 %copy-start.16 = (f32[320]{0:T(512)S(1)}, f32[320]{0:T(512)}, u32[]{:S(2)}) copy-start(f32[320]{0:T(512)} %copy-done.15) | copy-start | bytes 3844
  74.9 22.1 %copy-start.3 = (bf16[128,128]{1,0:T(8,128)(2,1)S(1)}, bf16[128,128]{1,0:T(8,128)(2,1)}, u32[]{:S(2)}) copy-start(bf16[128,128]{1,0:T(8,128)(2,1)} %out_w_ref.2) | copy-start | bytes 98308
  75.0 22.1 %copy-start.5 = (f32[128]{0:T(128)S(1)}, f32[128]{0:T(128)}, u32[]{:S(2)}) copy-start(f32[128]{0:T(128)} %param.26) | copy-start | bytes 1540
  75.0 22.1 %copy-start.6 = (f32[128]{0:T(128)S(1)}, f32[128]{0:T(128)}, u32[]{:S(2)}) copy-start(f32[128]{0:T(128)} %param.27) | copy-start | bytes 1540
  97.0 0.8 copy-start
  97.9 0.7 copy-start.11
  102.3 17.7 %copy-start.13 = (f32[320,320]{1,0:T(8,128)S(1)}, f32[320,320]{1,0:T(8,128)}, u32[]{:S(2)}) copy-start(f32[320,320]{1,0:T(8,128)} %compare_convert_fusion) | copy-start | bytes 1228804
  102.3 17.7 %copy-start.14 = (f32[320]{0:T(512)S(1)}, f32[320]{0:T(512)}, u32[]{:S(2)}) copy-start(f32[320]{0:T(512)} %add_multiply_fusion) | copy-start | bytes 3844
  102.3 17.7 %copy-start.19 = (f32[4]{0:T(128)S(1)}, f32[4]{0:T(128)}, u32[]{:S(2)}) copy-start(f32[4]{0:T(128)} %param.30) | copy-start | bytes 52
  120.3 0.9 copy-start.1
  120.3 0.9 copy-start.4

commit v4 on v3

--- a/solution.py
+++ b/solution.py
@@ -88,6 +88,8 @@
 
 
 def attention_kernel(
+    nr,
+    columns,
     mid_ref,
     extra_ref,
     valid_i_ref,
@@ -96,8 +98,35 @@
     shift_ref,
     qkvg_ref,
     out_w_ref,
-    result_ref,
+    out,
+    result,
+    own_sem,
+    send,
+    recv,
 ):
+    column = pl.program_id(0)
+    r, q = lax.axis_index("row"), lax.axis_index("col")
+    peers = [(lax.rem(r + e, nr), q) for e in range(1, nr)]
+    barrier = pltpu.get_barrier_semaphore()
+
+    def copies(c):
+        return [
+            pltpu.make_async_remote_copy(
+                src_ref=result.at[c, peer[0]],
+                dst_ref=out.at[r, c],
+                send_sem=send.at[e, c],
+                recv_sem=recv.at[e, c],
+                device_id=peer,
+                device_id_type=MESH,
+            )
+            for e, peer in enumerate(peers)
+        ] + [pltpu.make_async_copy(result.at[c, r], out.at[r, c], own_sem.at[c])]
+
+    @pl.when(column == 0)
+    def _():
+        for peer in peers:
+            pl.semaphore_signal(barrier, inc=1, device_id=peer, device_id_type=MESH)
+
     width = H * DH
     mid = mid_ref[0].astype(F32)
     att = layer_norm(mid, gain_ref[...], shift_ref[...]).astype(BF16)
@@ -127,7 +156,21 @@
     gated = (gate * sums[:, :width] / sums[:, width:]).astype(BF16)
     update = dot_nn(gated, out_w_ref[...])
     mask = valid_i_ref[...] * valid_j_ref[0]
-    result_ref[0] = (mid + mask * update).astype(BF16)
+    rows = mid.shape[0] // nr
+    result[column] = (mid + mask * update).astype(BF16).reshape(nr, rows, mid.shape[1])
+
+    @pl.when(column == 0)
+    def _():
+        pl.semaphore_wait(barrier, len(peers))
+
+    for copy in copies(column):
+        copy.start()
+
+    @pl.when(column == columns - 1)
+    def _():
+        for c in range(columns):
+            for copy in copies(c):
+                copy.wait()
 
 
 def greet(peers):
@@ -137,48 +180,63 @@
     pl.semaphore_wait(barrier, len(peers))
 
 
-def gather_kernel(nr, nq, src, out, own_sem, col_send, col_recv, row_send, row_recv):
+def gather_kernel(
+    nr, nq, src, out, own_sem, col_send, col_recv, row_send, row_recv, mate_send, mate_recv
+):
     r, q = lax.axis_index("row"), lax.axis_index("col")
     row_peers = [(lax.rem(r + e, nr), q) for e in range(1, nr)]
-    col_peers = [(r, lax.rem(q + d, nq)) for d in range(1, nq)]
-    greet(row_peers + col_peers)
+    col_peers = [(r, lax.rem(q + 2 * d, nq)) for d in range(1, nq // 2)]
+    mate = (r, q + 1 - 2 * lax.rem(q, 2))
+    greet(row_peers + col_peers + [mate])
+
+    def send(block, place, send_sem, recv_sem, peer):
+        copy = pltpu.make_async_remote_copy(
+            src_ref=block,
+            dst_ref=out.at[place[0], place[1]],
+            send_sem=send_sem,
+            recv_sem=recv_sem,
+            device_id=peer,
+            device_id_type=MESH,
+        )
+        copy.start()
+        return copy
+
+    over_col = [
+        send(src, (q, r), col_send.at[d], col_recv.at[d], peer) for d, peer in enumerate(col_peers)
+    ]
     own = pltpu.make_async_copy(src, out.at[q, r], own_sem)
     own.start()
-    over_col = []
-    for d in range(1, nq):
-        over_col.append(
-            pltpu.make_async_remote_copy(
-                src_ref=src,
-                dst_ref=out.at[q, r],
-                send_sem=col_send.at[d - 1],
-                recv_sem=col_recv.at[d - 1],
-                device_id=col_peers[d - 1],
-                device_id_type=MESH,
-            )
-        )
-        over_col[-1].start()
-    over_row = []
-    for d in range(nq):
-        source = lax.rem(q + nq - d, nq)
+    over_row, to_mate = [], []
+    for d in range(nq // 2):
+        source = lax.rem(q + nq - 2 * d, nq)
         block = src if d == 0 else out.at[source, r]
         if d > 0:
             over_col[d - 1].wait_recv()
-        for e in range(1, nr):
-            over_row.append(
-                pltpu.make_async_remote_copy(
-                    src_ref=block,
-                    dst_ref=out.at[source, r],
-                    send_sem=row_send.at[e - 1, d],
-                    recv_sem=row_recv.at[e - 1, d],
-                    device_id=row_peers[e - 1],
-                    device_id_type=MESH,
+        over_row.append(
+            [
+                send(block, (source, r), row_send.at[e, d], row_recv.at[e, d], peer)
+                for e, peer in enumerate(row_peers)
+            ]
+        )
+        to_mate.append(send(block, (source, r), mate_send.at[0, d], mate_recv.at[0, d], mate))
+    for d in range(nq // 2):
+        source = lax.rem(q + nq - 2 * d, nq)
+        for e in range(nr - 1):
+            over_row[d][e].wait_recv()
+            place = (source, lax.rem(r + nr - 1 - e, nr))
+            to_mate.append(
+                send(
+                    out.at[place[0], place[1]],
+                    place,
+                    mate_send.at[e + 1, d],
+                    mate_recv.at[e + 1, d],
+                    mate,
                 )
             )
-            over_row[-1].start()
     own.wait()
-    for copy in over_row:
-        copy.wait_recv()
-    for copy in over_col + over_row:
+    for copy in to_mate:
+        copy.wait()
+    for copy in over_col + sum(over_row, []):
         copy.wait_send()
 
 
@@ -190,57 +248,17 @@
         out_specs=pl.BlockSpec(memory_space=pltpu.VMEM),
         scratch_shapes=[
             pltpu.SemaphoreType.DMA,
-            pltpu.SemaphoreType.DMA((nq - 1,)),
-            pltpu.SemaphoreType.DMA((nq - 1,)),
-            pltpu.SemaphoreType.DMA((nr - 1, nq)),
-            pltpu.SemaphoreType.DMA((nr - 1, nq)),
+            pltpu.SemaphoreType.DMA((nq // 2 - 1,)),
+            pltpu.SemaphoreType.DMA((nq // 2 - 1,)),
+            pltpu.SemaphoreType.DMA((nr - 1, nq // 2)),
+            pltpu.SemaphoreType.DMA((nr - 1, nq // 2)),
+            pltpu.SemaphoreType.DMA((nr, nq // 2)),
+            pltpu.SemaphoreType.DMA((nr, nq // 2)),
         ],
         compiler_params=pltpu.CompilerParams(
             collective_id=0, has_side_effects=True, vmem_limit_bytes=VMEM_LIMIT
         ),
     )(block)
-
-
-def swap_kernel(nr, src, out, own_sem, send, recv):
-    r, q = lax.axis_index("row"), lax.axis_index("col")
-    peers = [(lax.rem(r + e, nr), q) for e in range(1, nr)]
-    greet(peers)
-    copies = []
-    for e in range(1, nr):
-        copies.append(
-            pltpu.make_async_remote_copy(
-                src_ref=src.at[:, peers[e - 1][0]],
-                dst_ref=out.at[r],
-                send_sem=send.at[e - 1],
-                recv_sem=recv.at[e - 1],
-                device_id=peers[e - 1],
-                device_id_type=MESH,
-            )
-        )
-        copies[-1].start()
-    own = pltpu.make_async_copy(src.at[:, r], out.at[r], own_sem)
-    own.start()
-    own.wait()
-    for copy in copies:
-        copy.wait()
-
-
-def swap_rows(array, nr):
-    shape = (array.shape[1], array.shape[0]) + array.shape[2:]
-    return pl.pallas_call(
-        functools.partial(swap_kernel, nr),
-        out_shape=jax.ShapeDtypeStruct(shape, array.dtype),
-        in_specs=[pl.BlockSpec(memory_space=pltpu.VMEM)],
-        out_specs=pl.BlockSpec(memory_space=pltpu.VMEM),
-        scratch_shapes=[
-            pltpu.SemaphoreType.DMA,
-            pltpu.SemaphoreType.DMA((nr - 1,)),
-            pltpu.SemaphoreType.DMA((nr - 1,)),
-        ],
-        compiler_params=pltpu.CompilerParams(
-            collective_id=2, has_side_effects=True, vmem_limit_bytes=VMEM_LIMIT
-        ),
-    )(array)
 
 
 def spread_kernel(nr, nq, sides, pair, spread, strip, own_sem, send, recv, row_send, row_recv):
@@ -311,18 +329,40 @@
     )(sides, pair)
 
 
+def cut_spec(shape, dim, steps):
+    block = tuple(n // steps if d == dim else n for d, n in enumerate(shape))
+    return pl.BlockSpec(block, lambda c: tuple(c if d == dim else 0 for d in range(len(shape))))
+
+
 def step_call(kernel, steps, ins, outs):
-    def spec(shape, dim):
-        block = tuple(n // steps if d == dim else n for d, n in enumerate(shape))
-        return pl.BlockSpec(block, lambda c: tuple(c if d == dim else 0 for d in range(len(shape))))
-
     return pl.pallas_call(
         kernel,
         grid=(steps,),
-        in_specs=[spec(a.shape, dim) for a, dim in ins],
-        out_specs=[spec(shape, dim) for shape, _, dim in outs],
+        in_specs=[cut_spec(a.shape, dim, steps) for a, dim in ins],
+        out_specs=[cut_spec(shape, dim, steps) for shape, _, dim in outs],
         out_shape=[jax.ShapeDtypeStruct(shape, t) for shape, t, _ in outs],
         compiler_params=pltpu.CompilerParams(vmem_limit_bytes=VMEM_LIMIT),
+    )(*[a for a, _ in ins])
+
+
+def attend_and_return(ins, nr):
+    columns, residues, channels = ins[0][0].shape
+    block = (residues // nr, channels)
+    return pl.pallas_call(
+        functools.partial(attention_kernel, nr, columns),
+        grid=(columns,),
+        in_specs=[cut_spec(a.shape, dim, columns) for a, dim in ins],
+        out_specs=pl.BlockSpec(memory_space=pl.ANY),
+        out_shape=jax.ShapeDtypeStruct((nr, columns) + block, BF16),
+        scratch_shapes=[
+            pltpu.VMEM((columns, nr) + block, BF16),
+            pltpu.SemaphoreType.DMA((columns,)),
+            pltpu.SemaphoreType.DMA((nr - 1, columns)),
+            pltpu.SemaphoreType.DMA((nr - 1, columns)),
+        ],
+        compiler_params=pltpu.CompilerParams(
+            collective_id=2, has_side_effects=True, vmem_limit_bytes=VMEM_LIMIT
+        ),
     )(*[a for a, _ in ins])
 
 
@@ -437,9 +477,7 @@
         + (MASK_NEG * (residue_valid - 1.0))[None, None, :]
     )
     extra = jnp.pad(extra, ((0, 0), (0, 0), (0, -residues % 128)), constant_values=FILLED)
-    (result,) = step_call(
-        attention_kernel,
-        strip,
+    result = attend_and_return(
         [
             (mid, 0),
             (extra, None),
@@ -450,10 +488,7 @@
             (qkvg_weight, None),
             (att_out_weight, None),
         ],
-        [((strip, residues, channels), BF16, 0)],
-    )
-    result = swap_rows(
-        result.reshape(strip, row_devices, row_count, channels), row_devices
+        row_devices,
     ).reshape(col_count, row_count, channels)
     return jnp.swapaxes(result, 0, 1)
 

time: 149 us -> 138 us (0.926)
  Pallas kernels: 89.4 us -> 78.7 us
    pallas_call x5 -> x4, Pallas kernels: 35.1 us -> 29.5 us  [the longest x1 20.7 us: attend_and_return(): pl.pallas_call(functools.partial(attention_kernel, nr, columns), grid=(co...]
    pallas_call x1, Pallas kernels: 17.3 us -> 12.2 us  [gather_all(): pl.pallas_call(functools.partial(gather_kernel, nr, nq), out_shape=jax.Sh...]
where the time goes in v4:
time: 138 us
  Pallas kernels  78.7 us (57%)
  local copies, waits for them, and re-layouts  25 us (18%)
  waiting for transfers between devices  16.9 us (12%)
  starting transfers between devices  12 us (9%)
  other arithmetic  2.89 us (2%)
  matrix products  2.01 us (1%)
    pallas_call x1, Pallas kernels, spread_all(): pl.pallas_call(functools.partial(spread_kernel, nr, nq), out_shape=[jax.S...  37 us
    pallas_call x1, Pallas kernels, attend_and_return(): pl.pallas_call(functools.partial(attention_kernel, nr, columns), grid=(co...  20.7 us
    all_to_all x1, waiting for transfers between devices, on_device(): lax.all_to_all(product, axes, split_axis=0, concat_axis=0, tiled=True)  16.9 us
    pallas_call x1, Pallas kernels, gather_all(): pl.pallas_call(functools.partial(gather_kernel, nr, nq), out_shape=jax.Sh...  12.2 us
    all_to_all x1, starting transfers between devices, on_device(): lax.all_to_all(product, axes, split_axis=0, concat_axis=0, tiled=True)  12 us
    reshape x2, local copies, waits for them, and re-layouts, on_device(): spread.reshape(col_devices, row_devices, 2, share, col_count, row_count)  8.97 us
    pallas_call x3, Pallas kernels, step_call(): pl.pallas_call(kernel, grid=(steps,), in_specs=[cut_spec(a.shape, dim, st...  8.79 us
    unnamed x44, local copies, waits for them, and re-layouts  4.65 us
  transfers between devices with their start and end apart: 1, of which 1 were waited for; matrix products, arithmetic and copies ran while one was open for 2% of the time, Pallas kernels for 1%

profile of v4, /device:TPU:0, one launch (start us, length us, event | category | flops | bytes accessed | tf_op | source)
XLA Modules:
  0.0 137.9 jit_solution(13687890324429216748)
XLA Ops:
  0.0 1.3 copy.49
  2.4 1.0 copy.28
  3.5 3.1 %shard_map.154 = bf16[256,3200]{1,0:T(8,128)(2,1)S(1)} custom-call(bf16[40,80,128]{2,1,0:T(8,128)(2,1)S(1)} %bitcast.38, f32[1,3200]{1,0:T(1,128)S(1)} %mul.61.mask_ref, f32[1,128]{1,0:T(1,128)S(1)} %bitcast.49, f32[1,128]{1,0:T(1,128)S(1)} %bitcast.51, bf16[512,128]{1,0:T(8,128)(2,1)S(1)} %bitcast.44), custom_call_target="tpu_custom_call" | custom-call | tf_op jit(solution)/shard_map/pallas_call | solution.py:338
  6.6 37.0 %shard_map.155 = (bf16[32,8,3200]{2,1,0:T(8,128)(2,1)S(1)}, bf16[10,4,80,128]{3,2,1,0:T(8,128)(2,1)S(1)}) custom-call(bf16[32,8,3200]{2,1,0:T(8,128)(2,1)S(1)} %bitcast.40, bf16[4,10,80,128]{3,2,1,0:T(8,128)(2,1)S(1)} %bitcast.39), custom_call_target="tpu_custom_call" | custom-call | tf_op jit(solution)/shard_map/pallas_call | solution.py:311
  43.7 3.9 %reshape.120 = bf16[8,4,2,4,40,80]{5,4,3,2,1,0:T(8,128)(2,1)} reshape(bf16[32,8,3200]{2,1,0:T(8,128)(2,1)S(1)} %get-tuple-element.10) | data formatting | bytes 3276800 | tf_op jit(solution)/shard_map/reshape | solution.py:447
  47.5 5.1 %copy.46 = bf16[8,4,2,4,40,80]{5,1,4,0,3,2:T(4,128)(2,1)S(1)} copy(bf16[8,4,2,4,40,80]{5,4,3,2,1,0:T(8,128)(2,1)} %reshape.120) | data formatting | bytes 3276800 | tf_op jit(solution)/shard_map/reshape | solution.py:447
  52.6 0.9 fusion.1
  53.6 1.7 %squeeze.6 = bf16[4,320,320]{2,1,0:T(8,128)(2,1)} reshape(bf16[1,4,8,40,4,80]{5,4,3,2,1,0:T(4,128)(2,1)S(1)} %get-tuple-element.14) | data formatting | bytes 1638400 | tf_op jit(solution)/shard_map/squeeze | solution.py:452
  55.3 1.7 %squeeze.7 = bf16[4,320,320]{2,1,0:T(8,128)(2,1)} reshape(bf16[1,4,8,40,4,80]{5,4,3,2,1,0:T(4,128)(2,1)S(1)} %get-tuple-element.13) | data formatting | bytes 1638400 | tf_op jit(solution)/shard_map/squeeze | solution.py:452
  57.0 2.0 %convolution_convert_fusion = bf16[4,320,320]{2,1,0:T(8,128)(2,1)S(1)} fusion(bf16[4,320,320]{2,1,0:T(8,128)(2,1)S(1)} %copy-done.12, bf16[4,320,320]{2,1,0:T(8,128)(2,1)} %squeeze.7), kind=kOutput, calls=%fused_computation.3 | convolution fusion | flops 262553600 | bytes 2457600 | tf_op jit(solution)/shard_map/cki,ckj->cji/dot_general | solution.py:451
  59.0 1.1 reshape.121
  60.2 1.3 copy.48
  61.5 12.0 %all-to-all-start = ((bf16[32,4,3200]{2,1,0:T(4,128)(2,1)}), bf16[32,4,3200]{2,1,0:T(4,128)(2,1)}, u32[]{:S(2)}, u32[]{:S(2)}) async-start(bf16[32,4,3200]{2,1,0:T(4,128)(2,1)} %bitcast.37), calls=%async_computation | async-start | bytes 1638400 | tf_op jit(solution)/shard_map/all_to_all | solution.py:455
  73.9 0.7 copy.34.out_shift_ref
  75.0 2.0 %shard_map.156.gate_ref = f32[10,320,128]{2,1,0:T(8,128)S(1)} custom-call(bf16[10,320,128]{2,1,0:T(8,128)(2,1)S(1)} %bitcast.41, f32[1,128]{1,0:T(1,128)S(1)} %bitcast.50, f32[1,128]{1,0:T(1,128)S(1)} %bitcast.52, bf16[128,128]{1,0:T(8,128)(2,1)S(1)} %copy-done.2), custom_call_target="tpu_custom_call" | custom-call | tf_op jit(solution)/shard_map/pallas_call | solution.py:338
  77.6 0.9 compare_convert_fusion
  78.5 16.9 %all-to-all-done = bf16[32,4,3200]{2,1,0:T(4,128)(2,1)} async-done(((bf16[32,4,3200]{2,1,0:T(4,128)(2,1)}), bf16[32,4,3200]{2,1,0:T(4,128)(2,1)}, u32[]{:S(2)}, u32[]{:S(2)}) %all-to-all-start) | async-done | bytes 819232 | tf_op jit(solution)/shard_map/all_to_all | solution.py:455
  95.4 1.6 %reshape.122.product_ref = bf16[128,3200]{1,0:T(8,128)(2,1)S(1)} reshape(bf16[32,4,3200]{2,1,0:T(4,128)(2,1)} %all-to-all-done) | data formatting | bytes 1638400 | tf_op jit(solution)/shard_map/reshape | solution.py:461
  97.1 0.8 copy-done
  98.6 3.7 %shard_map.157 = (bf16[10,320,128]{2,1,0:T(8,128)(2,1)S(1)}, bf16[10,4,320]{2,1,0:T(4,128)(2,1)S(1)}) custom-call(bf16[10,320,128]{2,1,0:T(8,128)(2,1)S(1)} %bitcast.42, bf16[128,3200]{1,0:T(8,128)(2,1)S(1)} %reshape.122.product_ref, f32[10,320,128]{2,1,0:T(8,128)S(1)} %shard_map.156.gate_ref, f32[128,1]{1,0:T(8,128)S(1)} %copy.33.out_gain_ref, ...), custom_call_target="tpu_custom_call" | custom-call | tf_op jit(solution)/shard_map/pallas_call | solution.py:338
  102.3 12.2 %shard_map.158 = bf16[8,4,10,4,320]{4,3,2,1,0:T(4,128)(2,1)S(1)} custom-call(bf16[10,4,320]{2,1,0:T(4,128)(2,1)S(1)} %get-tuple-element.12.src), custom_call_target="tpu_custom_call" | custom-call | tf_op jit(solution)/shard_map/pallas_call | solution.py:244
  115.4 0.7 copy-done.1
  116.1 20.7 %shard_map.159 = bf16[4,10,80,128]{3,2,1,0:T(8,128)(2,1)S(1)} custom-call(bf16[10,320,128]{2,1,0:T(8,128)(2,1)S(1)} %get-tuple-element.11.mid_ref, f32[4,320,384]{2,1,0:T(8,128)S(1)} %pad.4.extra_ref, f32[320,1]{1,0:T(8,128)S(1)} %convert_element_type.51.valid_i_ref, f32[10,1,1]{2,1,0:T(1,128)S(1)} %copy.37.valid_j_ref, f32[1,128]{1,0:T(1,128)S(1)} %bitcast.46, ...), custom_call_target="tpu_custom_call" | custom-call | tf_op jit(solution)/shard_map/pallas_call | solution.py:351
  136.8 1.1 copy.47
  (58 shorter events, 3.9 us)
Async XLA Ops:
  0.0 3.5 %copy-start.7 = (f32[128]{0:T(128)S(1)}, f32[128]{0:T(128)}, u32[]{:S(2)}) copy-start(f32[128]{0:T(128)} %param.19) | copy-start | bytes 1540
  0.0 3.5 %copy-start.9 = (f32[128]{0:T(128)S(1)}, f32[128]{0:T(128)}, u32[]{:S(2)}) copy-start(f32[128]{0:T(128)} %param.20) | copy-start | bytes 1540
  2.1 72.7 %copy-start.15 = (f32[320]{0:T(512)}, f32[320]{0:T(512)S(1)}, u32[]{:S(2)}) copy-start(f32[320]{0:T(512)S(1)} %convert_element_type.42) | copy-start | bytes 3844
  55.3 1.7 %copy-start.12 = (bf16[4,320,320]{2,1,0:T(8,128)(2,1)S(1)}, bf16[4,320,320]{2,1,0:T(8,128)(2,1)}, u32[]{:S(2)}) copy-start(bf16[4,320,320]{2,1,0:T(8,128)(2,1)} %squeeze.6) | copy-start | bytes 2457604
  60.1 13.6 %copy-start.17 = (f32[128]{0:T(128)S(1)}, f32[128]{0:T(128)}, u32[]{:S(2)}) copy-start(f32[128]{0:T(128)} %param.23) | copy-start | bytes 1540
  60.2 13.7 %copy-start.18 = (f32[128]{0:T(128)S(1)}, f32[128]{0:T(128)}, u32[]{:S(2)}) copy-start(f32[128]{0:T(128)} %param.24) | copy-start | bytes 1540
  60.2 14.4 %copy-start.20 = (s32[5]{0:T(128)S(1)}, s32[5]{0:T(128)}, u32[]{:S(2)}) copy-start(s32[5]{0:T(128)} %param.17) | copy-start | bytes 64
  60.2 14.8 %copy-start.2 = (bf16[128,128]{1,0:T(8,128)(2,1)S(1)}, bf16[128,128]{1,0:T(8,128)(2,1)}, u32[]{:S(2)}) copy-start(bf16[128,128]{1,0:T(8,128)(2,1)} %gate_w_ref.1) | copy-start | bytes 98308
  60.2 14.7 %copy-start.8 = (f32[128]{0:T(128)S(1)}, f32[128]{0:T(128)}, u32[]{:S(2)}) copy-start(f32[128]{0:T(128)} %param.19) | copy-start | bytes 1540
  60.2 14.7 %copy-start.10 = (f32[128]{0:T(128)S(1)}, f32[128]{0:T(128)}, u32[]{:S(2)}) copy-start(f32[128]{0:T(128)} %param.20) | copy-start | bytes 1540
  61.5 33.9 %all-to-all-start = ((bf16[32,4,3200]{2,1,0:T(4,128)(2,1)}), bf16[32,4,3200]{2,1,0:T(4,128)(2,1)}, u32[]{:S(2)}, u32[]{:S(2)}) async-start(bf16[32,4,3200]{2,1,0:T(4,128)(2,1)} %bitcast.37), calls=%async_computation | async-start | bytes 1638400 | tf_op jit(solution)/shard_map/all_to_all | solution.py:455
  74.8 2.1 %copy-start.16 = (f32[320]{0:T(512)S(1)}, f32[320]{0:T(512)}, u32[]{:S(2)}) copy-start(f32[320]{0:T(512)} %copy-done.15) | copy-start | bytes 3844
  74.9 22.1 %copy-start.3 = (bf16[128,128]{1,0:T(8,128)(2,1)S(1)}, bf16[128,128]{1,0:T(8,128)(2,1)}, u32[]{:S(2)}) copy-start(bf16[128,128]{1,0:T(8,128)(2,1)} %out_w_ref.2) | copy-start | bytes 98308
  75.0 22.1 %copy-start.5 = (f32[128]{0:T(128)S(1)}, f32[128]{0:T(128)}, u32[]{:S(2)}) copy-start(f32[128]{0:T(128)} %param.26) | copy-start | bytes 1540
  75.0 22.1 %copy-start.6 = (f32[128]{0:T(128)S(1)}, f32[128]{0:T(128)}, u32[]{:S(2)}) copy-start(f32[128]{0:T(128)} %param.27) | copy-start | bytes 1540
  97.0 0.8 copy-start
  97.9 0.7 copy-start.11
  102.3 12.6 %copy-start.13 = (f32[320,320]{1,0:T(8,128)S(1)}, f32[320,320]{1,0:T(8,128)}, u32[]{:S(2)}) copy-start(f32[320,320]{1,0:T(8,128)} %compare_convert_fusion) | copy-start | bytes 1228804
  102.3 12.6 %copy-start.14 = (f32[320]{0:T(512)S(1)}, f32[320]{0:T(512)}, u32[]{:S(2)}) copy-start(f32[320]{0:T(512)} %add_multiply_fusion) | copy-start | bytes 3844
  102.3 12.6 %copy-start.19 = (f32[4]{0:T(128)S(1)}, f32[4]{0:T(128)}, u32[]{:S(2)}) copy-start(f32[4]{0:T(128)} %param.30) | copy-start | bytes 52
  115.2 0.9 copy-start.1
  115.2 0.9 copy-start.4

commit v5 on v4

--- a/solution.py
+++ b/solution.py
@@ -54,6 +54,27 @@
     normed = layer_norm(flat, gain_ref[...], shift_ref[...]).astype(BF16)
     gate = jax.nn.sigmoid(dot_nn(normed, gate_w_ref[...]))
     gate_ref[...] = gate.reshape(columns, rows, channels)
+
+
+def product_kernel(spread_ref, product_ref, ordered):
+    step = pl.program_id(0)
+    nr, sides, flat = spread_ref.shape
+    share, residues = product_ref.shape[:2]
+    rows = residues // nr
+    count = flat // rows
+    parts = [spread_ref[r].astype(F32) for r in range(nr)]
+    lines = [
+        jnp.concatenate([part[:, k * rows : (k + 1) * rows] for part in parts], axis=1)
+        for k in range(count)
+    ]
+    block = jnp.swapaxes(jnp.stack(lines, axis=0), 0, 1)
+    ordered[:, pl.ds(pl.multiple_of(step * count, 8), count), :] = block
+
+    @pl.when(step == residues // count - 1)
+    def _():
+        for channel in range(share):
+            left, right = ordered[channel].astype(BF16), ordered[share + channel].astype(BF16)
+            product_ref[channel] = dot_tn(right, left).astype(BF16)
 
 
 def middle_kernel(
@@ -443,14 +464,15 @@
         ],
         [((strip, residues, channels), F32, 0)],
     )
-    spread = (
-        spread.reshape(col_devices, row_devices, 2, share, col_count, row_count)
-        .transpose(2, 3, 0, 4, 1, 5)
-        .reshape(2, share, residues, residues)
-    )
-    product = jnp.einsum(
-        "cki,ckj->cji", spread[0], spread[1], preferred_element_type=F32
-    ).astype(BF16)
+    product = pl.pallas_call(
+        product_kernel,
+        grid=(col_devices,),
+        in_specs=[cut_spec(spread.shape, 0, col_devices)],
+        out_specs=cut_spec((share, residues, residues), None, col_devices),
+        out_shape=jax.ShapeDtypeStruct((share, residues, residues), BF16),
+        scratch_shapes=[pltpu.VMEM((2 * share, residues, residues), F32)],
+        compiler_params=pltpu.CompilerParams(vmem_limit_bytes=VMEM_LIMIT),
+    )(spread)
     product = jnp.swapaxes(product.reshape(share, devices, flat), 0, 1)
     product = lax.all_to_all(product, axes, split_axis=0, concat_axis=0, tiled=True)
     mid, bias = step_call(

time: 138 us -> 126 us (0.913)
  local copies, waits for them, and re-layouts: 25 us -> 11.7 us
  Pallas kernels: 78.7 us -> 81.8 us
  matrix products: 2.01 us -> 0 us
    reshape x2 -> x0, local copies, waits for them, and re-layouts: 8.97 us -> none  [on_device(): spread.reshape(col_devices, row_devices, 2, share, col_count, row_count)]
    squeeze x2 -> x0, local copies, waits for them, and re-layouts: 3.37 us -> none  [the longest x1 1.69 us: on_device(): spread[0]]
    pallas_call x0 -> x1, Pallas kernels: none -> 2.62 us  [on_device(): pl.pallas_call(product_kernel, grid=(col_devices,), in_specs=[cut_spec(sp...]
    dot_general x1 -> x0, matrix products: 2.01 us -> none  [on_device(): jnp.einsum('cki,ckj->cji', spread[0], spread[1], preferred_element_type=F32)]
    unnamed x44 -> x38, local copies, waits for them, and re-layouts: 4.65 us -> 4.63 us
  transfers between devices with their start and end apart: 1 -> 1, of which waited for: 1 -> 1; matrix products, arithmetic and copies ran while one was open for 2% -> 2% of each run, Pallas kernels for 1% -> 2%
where the time goes in v5:
time: 126 us
  Pallas kernels  81.8 us (65%)
  waiting for transfers between devices  17.1 us (14%)
  starting transfers between devices  11.9 us (9%)
  local copies, waits for them, and re-layouts  11.7 us (9%)
  other arithmetic  2.88 us (2%)
    pallas_call x1, Pallas kernels, spread_all(): pl.pallas_call(functools.partial(spread_kernel, nr, nq), out_shape=[jax.S...  37 us
    pallas_call x1, Pallas kernels, attend_and_return(): pl.pallas_call(functools.partial(attention_kernel, nr, columns), grid=(co...  21.1 us
    all_to_all x1, waiting for transfers between devices, on_device(): lax.all_to_all(product, axes, split_axis=0, concat_axis=0, tiled=True)  17.1 us
    pallas_call x1, Pallas kernels, gather_all(): pl.pallas_call(functools.partial(gather_kernel, nr, nq), out_shape=jax.Sh...  12.2 us
    all_to_all x1, starting transfers between devices, on_device(): lax.all_to_all(product, axes, split_axis=0, concat_axis=0, tiled=True)  11.9 us
    pallas_call x3, Pallas kernels, step_call(): pl.pallas_call(kernel, grid=(steps,), in_specs=[cut_spec(a.shape, dim, st...  8.79 us
    unnamed x38, local copies, waits for them, and re-layouts  4.63 us
    pallas_call x1, Pallas kernels, on_device(): pl.pallas_call(product_kernel, grid=(col_devices,), in_specs=[cut_spec(sp...  2.62 us
  transfers between devices with their start and end apart: 1, of which 1 were waited for; matrix products, arithmetic and copies ran while one was open for 2% of the time, Pallas kernels for 2%

profile of v5, /device:TPU:0, one launch (start us, length us, event | category | flops | bytes accessed | tf_op | source)
XLA Modules:
  0.0 125.6 jit_solution(699651030732402205)
XLA Ops:
  0.0 1.3 %copy.42 = bf16[80,40,128]{2,0,1:T(8,128)(2,1)S(1)} copy(bf16[80,40,128]{2,1,0:T(8,128)(2,1)} %param.16) | data formatting | bytes 1638400 | tf_op args[0]
  1.3 0.7 convert_element_type.38
  2.4 1.0 copy.26
  3.5 3.1 %shard_map.154 = bf16[256,3200]{1,0:T(8,128)(2,1)S(1)} custom-call(bf16[40,80,128]{2,1,0:T(8,128)(2,1)S(1)} %bitcast.33, f32[1,3200]{1,0:T(1,128)S(1)} %mul.61.mask_ref, f32[1,128]{1,0:T(1,128)S(1)} %bitcast.44, f32[1,128]{1,0:T(1,128)S(1)} %bitcast.46, bf16[512,128]{1,0:T(8,128)(2,1)S(1)} %bitcast.39), custom_call_target="tpu_custom_call" | custom-call | tf_op jit(solution)/shard_map/pallas_call | solution.py:359
  6.6 37.0 %shard_map.155 = (bf16[32,8,3200]{2,1,0:T(8,128)(2,1)S(1)}, bf16[10,4,80,128]{3,2,1,0:T(8,128)(2,1)S(1)}) custom-call(bf16[32,8,3200]{2,1,0:T(8,128)(2,1)S(1)} %bitcast.35, bf16[4,10,80,128]{3,2,1,0:T(8,128)(2,1)S(1)} %bitcast.34), custom_call_target="tpu_custom_call" | custom-call | tf_op jit(solution)/shard_map/pallas_call | solution.py:332
  43.7 2.6 %shard_map.156 = bf16[4,320,320]{2,1,0:T(8,128)(2,1)S(1)} custom-call(bf16[32,8,3200]{2,1,0:T(8,128)(2,1)S(1)} %get-tuple-element.10.spread_ref), custom_call_target="tpu_custom_call" | custom-call | tf_op jit(solution)/shard_map/pallas_call | solution.py:467
  46.3 1.1 reshape.112
  47.5 1.3 %copy.41 = bf16[4,32,3200]{2,0,1:T(4,128)(2,1)} copy(bf16[4,32,3200]{2,1,0:T(8,128)(2,1)S(1)} %reshape.112) | data formatting | bytes 1638400 | tf_op jit(solution)/shard_map/reshape | solution.py:476
  48.8 11.9 %all-to-all-start = ((bf16[32,4,3200]{2,1,0:T(4,128)(2,1)}), bf16[32,4,3200]{2,1,0:T(4,128)(2,1)}, u32[]{:S(2)}, u32[]{:S(2)}) async-start(bf16[32,4,3200]{2,1,0:T(4,128)(2,1)} %bitcast.32), calls=%async_computation | async-start | bytes 1638400 | tf_op jit(solution)/shard_map/all_to_all | solution.py:477
  61.0 0.7 copy.30.out_shift_ref
  62.0 2.0 %shard_map.157.gate_ref = f32[10,320,128]{2,1,0:T(8,128)S(1)} custom-call(bf16[10,320,128]{2,1,0:T(8,128)(2,1)S(1)} %bitcast.36, f32[1,128]{1,0:T(1,128)S(1)} %bitcast.45, f32[1,128]{1,0:T(1,128)S(1)} %bitcast.47, bf16[128,128]{1,0:T(8,128)(2,1)S(1)} %copy-done.2), custom_call_target="tpu_custom_call" | custom-call | tf_op jit(solution)/shard_map/pallas_call | solution.py:359
  64.0 0.6 add_multiply_fusion
  64.6 0.9 compare_convert_fusion
  65.5 17.1 %all-to-all-done = bf16[32,4,3200]{2,1,0:T(4,128)(2,1)} async-done(((bf16[32,4,3200]{2,1,0:T(4,128)(2,1)}), bf16[32,4,3200]{2,1,0:T(4,128)(2,1)}, u32[]{:S(2)}, u32[]{:S(2)}) %all-to-all-start) | async-done | bytes 819232 | tf_op jit(solution)/shard_map/all_to_all | solution.py:477
  82.7 1.6 %reshape.113.product_ref = bf16[128,3200]{1,0:T(8,128)(2,1)S(1)} reshape(bf16[32,4,3200]{2,1,0:T(4,128)(2,1)} %all-to-all-done) | data formatting | bytes 1638400 | tf_op jit(solution)/shard_map/reshape | solution.py:483
  84.3 0.8 copy-done
  85.2 0.7 copy-done.9
  85.8 3.7 %shard_map.158 = (bf16[10,320,128]{2,1,0:T(8,128)(2,1)S(1)}, bf16[10,4,320]{2,1,0:T(4,128)(2,1)S(1)}) custom-call(bf16[10,320,128]{2,1,0:T(8,128)(2,1)S(1)} %bitcast.37, bf16[128,3200]{1,0:T(8,128)(2,1)S(1)} %reshape.113.product_ref, f32[10,320,128]{2,1,0:T(8,128)S(1)} %shard_map.157.gate_ref, f32[128,1]{1,0:T(8,128)S(1)} %copy.29.out_gain_ref, ...), custom_call_target="tpu_custom_call" | custom-call | tf_op jit(solution)/shard_map/pallas_call | solution.py:359
  89.6 12.2 %shard_map.159 = bf16[8,4,10,4,320]{4,3,2,1,0:T(4,128)(2,1)S(1)} custom-call(bf16[10,4,320]{2,1,0:T(4,128)(2,1)S(1)} %get-tuple-element.12.src), custom_call_target="tpu_custom_call" | custom-call | tf_op jit(solution)/shard_map/pallas_call | solution.py:265
  101.8 0.4 bitcast_convert_fusion
  102.2 0.3 fusion
  102.6 0.7 copy-done.1
  103.4 21.1 %shard_map.160 = bf16[4,10,80,128]{3,2,1,0:T(8,128)(2,1)S(1)} custom-call(bf16[10,320,128]{2,1,0:T(8,128)(2,1)S(1)} %get-tuple-element.11.mid_ref, f32[4,320,384]{2,1,0:T(8,128)S(1)} %pad.4.extra_ref, f32[320,1]{1,0:T(8,128)S(1)} %convert_element_type.47.valid_i_ref, f32[10,1,1]{2,1,0:T(1,128)S(1)} %copy.33.valid_j_ref, f32[1,128]{1,0:T(1,128)S(1)} %bitcast.41, ...), custom_call_target="tpu_custom_call" | custom-call | tf_op jit(solution)/shard_map/pallas_call | solution.py:372
  124.5 1.1 copy.40
  (47 shorter events, 1.3 us)
Async XLA Ops:
  0.0 3.5 %copy-start.7 = (f32[128]{0:T(128)S(1)}, f32[128]{0:T(128)}, u32[]{:S(2)}) copy-start(f32[128]{0:T(128)} %param.19) | copy-start | bytes 1540
  0.0 3.5 %copy-start.8 = (f32[128]{0:T(128)S(1)}, f32[128]{0:T(128)}, u32[]{:S(2)}) copy-start(f32[128]{0:T(128)} %param.20) | copy-start | bytes 1540
  2.1 59.8 %copy-start.12 = (f32[320]{0:T(512)}, f32[320]{0:T(512)S(1)}, u32[]{:S(2)}) copy-start(f32[320]{0:T(512)S(1)} %convert_element_type.39) | copy-start | bytes 3844
  47.4 13.4 %copy-start.14 = (f32[128]{0:T(128)S(1)}, f32[128]{0:T(128)}, u32[]{:S(2)}) copy-start(f32[128]{0:T(128)} %param.23) | copy-start | bytes 1540
  47.5 13.5 %copy-start.15 = (f32[128]{0:T(128)S(1)}, f32[128]{0:T(128)}, u32[]{:S(2)}) copy-start(f32[128]{0:T(128)} %param.24) | copy-start | bytes 1540
  47.5 14.2 %copy-start.17 = (s32[5]{0:T(128)S(1)}, s32[5]{0:T(128)}, u32[]{:S(2)}) copy-start(s32[5]{0:T(128)} %param.17) | copy-start | bytes 64
  47.5 14.6 %copy-start.2 = (bf16[128,128]{1,0:T(8,128)(2,1)S(1)}, bf16[128,128]{1,0:T(8,128)(2,1)}, u32[]{:S(2)}) copy-start(bf16[128,128]{1,0:T(8,128)(2,1)} %gate_w_ref.1) | copy-start | bytes 98308
  48.8 33.9 %all-to-all-start = ((bf16[32,4,3200]{2,1,0:T(4,128)(2,1)}), bf16[32,4,3200]{2,1,0:T(4,128)(2,1)}, u32[]{:S(2)}, u32[]{:S(2)}) async-start(bf16[32,4,3200]{2,1,0:T(4,128)(2,1)} %bitcast.32), calls=%async_computation | async-start | bytes 1638400 | tf_op jit(solution)/shard_map/all_to_all | solution.py:477
  61.9 2.1 %copy-start.13 = (f32[320]{0:T(512)S(1)}, f32[320]{0:T(512)}, u32[]{:S(2)}) copy-start(f32[320]{0:T(512)} %copy-done.12) | copy-start | bytes 3844
  62.0 22.3 %copy-start.3 = (bf16[128,128]{1,0:T(8,128)(2,1)S(1)}, bf16[128,128]{1,0:T(8,128)(2,1)}, u32[]{:S(2)}) copy-start(bf16[128,128]{1,0:T(8,128)(2,1)} %out_w_ref.2) | copy-start | bytes 98308
  62.0 22.3 %copy-start.5 = (f32[128]{0:T(128)S(1)}, f32[128]{0:T(128)}, u32[]{:S(2)}) copy-start(f32[128]{0:T(128)} %param.26) | copy-start | bytes 1540
  62.0 22.3 %copy-start.6 = (f32[128]{0:T(128)S(1)}, f32[128]{0:T(128)}, u32[]{:S(2)}) copy-start(f32[128]{0:T(128)} %param.27) | copy-start | bytes 1540
  84.3 0.8 copy-start
  85.2 0.7 copy-start.9
  89.6 12.6 %copy-start.10 = (f32[320,320]{1,0:T(8,128)S(1)}, f32[320,320]{1,0:T(8,128)}, u32[]{:S(2)}) copy-start(f32[320,320]{1,0:T(8,128)} %compare_convert_fusion) | copy-start | bytes 1228804
  89.6 12.6 %copy-start.11 = (f32[320]{0:T(512)S(1)}, f32[320]{0:T(512)}, u32[]{:S(2)}) copy-start(f32[320]{0:T(512)} %add_multiply_fusion) | copy-start | bytes 3844
  89.6 12.6 %copy-start.16 = (f32[4]{0:T(128)S(1)}, f32[4]{0:T(128)}, u32[]{:S(2)}) copy-start(f32[4]{0:T(128)} %param.30) | copy-start | bytes 52
  102.5 0.9 copy-start.1
  102.5 0.9 copy-start.4

commit v6 on v5

--- a/solution.py
+++ b/solution.py
@@ -115,9 +115,8 @@
     extra_ref,
     valid_i_ref,
     valid_j_ref,
-    gain_ref,
-    shift_ref,
-    qkvg_ref,
+    qkv_ref,
+    gate_ref,
     out_w_ref,
     out,
     result,
@@ -150,12 +149,10 @@
 
     width = H * DH
     mid = mid_ref[0].astype(F32)
-    att = layer_norm(mid, gain_ref[...], shift_ref[...]).astype(BF16)
-    heads = dot_nn(att, qkvg_ref[...])
-    queries = (heads[:, :width] * DH ** (-0.5)).astype(BF16)
-    keys = heads[:, width : 2 * width].astype(BF16)
-    vals = heads[:, 2 * width : 3 * width].astype(BF16)
-    gate = jax.nn.sigmoid(heads[:, 3 * width :])
+    queries = qkv_ref[0, :, :width]
+    keys = qkv_ref[0, :, width : 2 * width]
+    vals = qkv_ref[0, :, 2 * width :]
+    gate = gate_ref[0]
     rows, padded = extra_ref.shape[1:]
     lane_head = lax.broadcasted_iota(jnp.int32, (rows, width), 1) // DH
     filler = jnp.zeros((padded - rows, width), BF16)
@@ -202,7 +199,23 @@
 
 
 def gather_kernel(
-    nr, nq, src, out, own_sem, col_send, col_recv, row_send, row_recv, mate_send, mate_recv
+    nr,
+    nq,
+    src,
+    mid_ref,
+    gain_ref,
+    shift_ref,
+    qkvg_ref,
+    out,
+    qkv_ref,
+    gate_ref,
+    own_sem,
+    col_send,
+    col_recv,
+    row_send,
+    row_recv,
+    mate_send,
+    mate_recv,
 ):
     r, q = lax.axis_index("row"), lax.axis_index("col")
     row_peers = [(lax.rem(r + e, nr), q) for e in range(1, nr)]
@@ -228,7 +241,20 @@
     own = pltpu.make_async_copy(src, out.at[q, r], own_sem)
     own.start()
     over_row, to_mate = [], []
+    width = H * DH
+    columns = mid_ref.shape[0]
+
+    def project(column, carry):
+        att = layer_norm(mid_ref[column].astype(F32), gain_ref[...], shift_ref[...]).astype(BF16)
+        heads = dot_nn(att, qkvg_ref[...])
+        qkv_ref[column, :, :width] = (heads[:, :width] * DH ** (-0.5)).astype(BF16)
+        qkv_ref[column, :, width:] = heads[:, width : 3 * width].astype(BF16)
+        gate_ref[column] = jax.nn.sigmoid(heads[:, 3 * width :])
+        return carry
+
     for d in range(nq // 2):
+        if d == 1:
+            lax.fori_loop(0, columns // 2, project, 0)
         source = lax.rem(q + nq - 2 * d, nq)
         block = src if d == 0 else out.at[source, r]
         if d > 0:
@@ -240,6 +266,7 @@
             ]
         )
         to_mate.append(send(block, (source, r), mate_send.at[0, d], mate_recv.at[0, d], mate))
+    lax.fori_loop(columns // 2, columns, project, 0)
     for d in range(nq // 2):
         source = lax.rem(q + nq - 2 * d, nq)
         for e in range(nr - 1):
@@ -261,12 +288,17 @@
         copy.wait_send()
 
 
-def gather_all(block, nr, nq):
+def gather_all(block, mid, gain, shift, qkvg, nr, nq):
+    width = H * DH
     return pl.pallas_call(
         functools.partial(gather_kernel, nr, nq),
-        out_shape=jax.ShapeDtypeStruct((nq, nr) + block.shape, block.dtype),
-        in_specs=[pl.BlockSpec(memory_space=pltpu.VMEM)],
-        out_specs=pl.BlockSpec(memory_space=pltpu.VMEM),
+        out_shape=[
+            jax.ShapeDtypeStruct((nq, nr) + block.shape, block.dtype),
+            jax.ShapeDtypeStruct(mid.shape[:2] + (3 * width,), BF16),
+            jax.ShapeDtypeStruct(mid.shape[:2] + (width,), F32),
+        ],
+        in_specs=[pl.BlockSpec(memory_space=pltpu.VMEM)] * 5,
+        out_specs=[pl.BlockSpec(memory_space=pltpu.VMEM)] * 3,
         scratch_shapes=[
             pltpu.SemaphoreType.DMA,
             pltpu.SemaphoreType.DMA((nq // 2 - 1,)),
@@ -279,7 +311,7 @@
         compiler_params=pltpu.CompilerParams(
             collective_id=0, has_side_effects=True, vmem_limit_bytes=VMEM_LIMIT
         ),
-    )(block)
+    )(block, mid, gain, shift, qkvg)
 
 
 def spread_kernel(nr, nq, sides, pair, spread, strip, own_sem, send, recv, row_send, row_recv):
@@ -491,7 +523,16 @@
         ],
         [((strip, residues, channels), BF16, 0), ((strip, H, residues), BF16, 0)],
     )
-    bias = gather_all(bias, row_devices, col_devices).reshape(residues, H, residues)
+    bias, qkv, gate = gather_all(
+        bias,
+        mid,
+        att_norm_gain[None, :],
+        att_norm_bias[None, :],
+        qkvg_weight,
+        row_devices,
+        col_devices,
+    )
+    bias = bias.reshape(residues, H, residues)
     crossing = (residue_chain[:, None] != residue_chain[None, :]).astype(F32)
     extra = (
         jnp.swapaxes(bias, 0, 1).astype(F32)
@@ -505,9 +546,8 @@
             (extra, None),
             (residue_valid[:, None], None),
             (valid_j[:, :, None], 0),
-            (att_norm_gain[None, :], None),
-            (att_norm_bias[None, :], None),
-            (qkvg_weight, None),
+            (qkv, 0),
+            (gate, 0),
             (att_out_weight, None),
         ],
         row_devices,

time: 126 us -> 123 us (0.976)
  Pallas kernels: 81.8 us -> 78.2 us
    pallas_call x1, Pallas kernels: 21.1 us -> 17.5 us  [attend_and_return(): pl.pallas_call(functools.partial(attention_kernel, nr, columns), grid=(co...]
    unnamed x38 -> x40, local copies, waits for them, and re-layouts: 4.63 us -> 5.55 us
where the time goes in v6:
time: 123 us
  Pallas kernels  78.2 us (64%)
  waiting for transfers between devices  17.2 us (14%)
  local copies, waits for them, and re-layouts  12.6 us (10%)
  starting transfers between devices  11.9 us (10%)
  other arithmetic  2.88 us (2%)
    pallas_call x1, Pallas kernels, spread_all(): pl.pallas_call(functools.partial(spread_kernel, nr, nq), out_shape=[jax.S...  37 us
    pallas_call x1, Pallas kernels, attend_and_return(): pl.pallas_call(functools.partial(attention_kernel, nr, columns), grid=(co...  17.5 us
    all_to_all x1, waiting for transfers between devices, on_device(): lax.all_to_all(product, axes, split_axis=0, concat_axis=0, tiled=True)  17.2 us
    pallas_call x1, Pallas kernels, gather_all(): pl.pallas_call(functools.partial(gather_kernel, nr, nq), out_shape=[jax.S...  12.2 us
    all_to_all x1, starting transfers between devices, on_device(): lax.all_to_all(product, axes, split_axis=0, concat_axis=0, tiled=True)  11.9 us
    pallas_call x3, Pallas kernels, step_call(): pl.pallas_call(kernel, grid=(steps,), in_specs=[cut_spec(a.shape, dim, st...  8.8 us
    unnamed x40, local copies, waits for them, and re-layouts  5.55 us
    pallas_call x1, Pallas kernels, on_device(): pl.pallas_call(product_kernel, grid=(col_devices,), in_specs=[cut_spec(sp...  2.62 us
  transfers between devices with their start and end apart: 1, of which 1 were waited for; matrix products, arithmetic and copies ran while one was open for 2% of the time, Pallas kernels for 2%

profile of v6, /device:TPU:0, one launch (start us, length us, event | category | flops | bytes accessed | tf_op | source)
XLA Modules:
  0.0 123.0 jit_solution(9817144232377790489)
XLA Ops:
  0.0 0.7 convert_element_type.38
  1.2 1.3 %copy.42 = bf16[80,40,128]{2,0,1:T(8,128)(2,1)S(1)} copy(bf16[80,40,128]{2,1,0:T(8,128)(2,1)} %param.16) | data formatting | bytes 1638400 | tf_op args[0]
  2.4 1.0 copy.26
  3.5 3.1 %shard_map.154 = bf16[256,3200]{1,0:T(8,128)(2,1)S(1)} custom-call(bf16[40,80,128]{2,1,0:T(8,128)(2,1)S(1)} %bitcast.33, f32[1,3200]{1,0:T(1,128)S(1)} %mul.61.mask_ref, f32[1,128]{1,0:T(1,128)S(1)} %bitcast.44, f32[1,128]{1,0:T(1,128)S(1)} %bitcast.46, bf16[512,128]{1,0:T(8,128)(2,1)S(1)} %bitcast.39), custom_call_target="tpu_custom_call" | custom-call | tf_op jit(solution)/shard_map/pallas_call | solution.py:391
  6.6 37.0 %shard_map.155 = (bf16[32,8,3200]{2,1,0:T(8,128)(2,1)S(1)}, bf16[10,4,80,128]{3,2,1,0:T(8,128)(2,1)S(1)}) custom-call(bf16[32,8,3200]{2,1,0:T(8,128)(2,1)S(1)} %bitcast.35, bf16[4,10,80,128]{3,2,1,0:T(8,128)(2,1)S(1)} %bitcast.34), custom_call_target="tpu_custom_call" | custom-call | tf_op jit(solution)/shard_map/pallas_call | solution.py:364
  43.7 2.6 %shard_map.156 = bf16[4,320,320]{2,1,0:T(8,128)(2,1)S(1)} custom-call(bf16[32,8,3200]{2,1,0:T(8,128)(2,1)S(1)} %get-tuple-element.13.spread_ref), custom_call_target="tpu_custom_call" | custom-call | tf_op jit(solution)/shard_map/pallas_call | solution.py:499
  46.3 1.1 reshape.112
  47.5 1.3 %copy.41 = bf16[4,32,3200]{2,0,1:T(4,128)(2,1)} copy(bf16[4,32,3200]{2,1,0:T(8,128)(2,1)S(1)} %reshape.112) | data formatting | bytes 1638400 | tf_op jit(solution)/shard_map/reshape | solution.py:508
  48.8 11.9 %all-to-all-start = ((bf16[32,4,3200]{2,1,0:T(4,128)(2,1)}), bf16[32,4,3200]{2,1,0:T(4,128)(2,1)}, u32[]{:S(2)}, u32[]{:S(2)}) async-start(bf16[32,4,3200]{2,1,0:T(4,128)(2,1)} %bitcast.32), calls=%async_computation | async-start | bytes 1638400 | tf_op jit(solution)/shard_map/all_to_all | solution.py:509
  61.0 0.7 copy.30.out_shift_ref
  62.0 2.0 %shard_map.157.gate_ref = f32[10,320,128]{2,1,0:T(8,128)S(1)} custom-call(bf16[10,320,128]{2,1,0:T(8,128)(2,1)S(1)} %bitcast.36, f32[1,128]{1,0:T(1,128)S(1)} %bitcast.45, f32[1,128]{1,0:T(1,128)S(1)} %bitcast.47, bf16[128,128]{1,0:T(8,128)(2,1)S(1)} %copy-done.3), custom_call_target="tpu_custom_call" | custom-call | tf_op jit(solution)/shard_map/pallas_call | solution.py:391
  64.0 0.6 add_multiply_fusion
  64.6 0.9 compare_convert_fusion
  65.5 17.2 %all-to-all-done = bf16[32,4,3200]{2,1,0:T(4,128)(2,1)} async-done(((bf16[32,4,3200]{2,1,0:T(4,128)(2,1)}), bf16[32,4,3200]{2,1,0:T(4,128)(2,1)}, u32[]{:S(2)}, u32[]{:S(2)}) %all-to-all-start) | async-done | bytes 819232 | tf_op jit(solution)/shard_map/all_to_all | solution.py:509
  82.7 1.6 %reshape.113.product_ref = bf16[128,3200]{1,0:T(8,128)(2,1)S(1)} reshape(bf16[32,4,3200]{2,1,0:T(4,128)(2,1)} %all-to-all-done) | data formatting | bytes 1638400 | tf_op jit(solution)/shard_map/reshape | solution.py:515
  84.3 0.8 copy-done.1
  85.2 0.7 copy-done.10
  85.8 3.7 %shard_map.158 = (bf16[10,320,128]{2,1,0:T(8,128)(2,1)S(1)}, bf16[10,4,320]{2,1,0:T(4,128)(2,1)S(1)}) custom-call(bf16[10,320,128]{2,1,0:T(8,128)(2,1)S(1)} %bitcast.37, bf16[128,3200]{1,0:T(8,128)(2,1)S(1)} %reshape.113.product_ref, f32[10,320,128]{2,1,0:T(8,128)S(1)} %shard_map.157.gate_ref, f32[128,1]{1,0:T(8,128)S(1)} %copy.29.out_gain_ref, ...), custom_call_target="tpu_custom_call" | custom-call | tf_op jit(solution)/shard_map/pallas_call | solution.py:391
  89.6 12.2 %shard_map.159 = (bf16[8,4,10,4,320]{4,3,2,1,0:T(4,128)(2,1)S(1)}, bf16[10,320,384]{2,1,0:T(8,128)(2,1)S(1)}, f32[10,320,128]{2,1,0:T(8,128)S(1)}) custom-call(bf16[10,4,320]{2,1,0:T(4,128)(2,1)S(1)} %get-tuple-element.15.src, bf16[10,320,128]{2,1,0:T(8,128)(2,1)S(1)} %get-tuple-element.14.mid_ref, f32[1,128]{1,0:T(1,128)S(1)} %bitcast.41, ...), custom_call_target="tpu_custom_call" | custom-call | tf_op jit(solution)/shard_map/pallas_call | solution.py:293
  101.8 0.4 bitcast_convert_fusion
  102.2 1.1 copy-done
  103.7 0.6 copy-done.5
  104.3 17.5 %shard_map.160 = bf16[4,10,80,128]{3,2,1,0:T(8,128)(2,1)S(1)} custom-call(bf16[10,320,128]{2,1,0:T(8,128)(2,1)S(1)} %get-tuple-element.14.mid_ref, f32[4,320,384]{2,1,0:T(8,128)S(1)} %pad.4.extra_ref, f32[320,1]{1,0:T(8,128)S(1)} %convert_element_type.47.valid_i_ref, f32[10,1,1]{2,1,0:T(1,128)S(1)} %copy.33.valid_j_ref, bf16[10,320,384]{2,1,0:T(8,128)(2,1)} %copy-done, ...), custom_call_target="tpu_custom_call" | custom-call | tf_op jit(solution)/shard_map/pallas_call | solution.py:404
  121.9 1.1 copy.40
  (49 shorter events, 1.6 us)
Async XLA Ops:
  0.0 3.5 %copy-start.8 = (f32[128]{0:T(128)S(1)}, f32[128]{0:T(128)}, u32[]{:S(2)}) copy-start(f32[128]{0:T(128)} %param.19) | copy-start | bytes 1540
  0.0 3.5 %copy-start.9 = (f32[128]{0:T(128)S(1)}, f32[128]{0:T(128)}, u32[]{:S(2)}) copy-start(f32[128]{0:T(128)} %param.20) | copy-start | bytes 1540
  0.8 61.0 %copy-start.13 = (f32[320]{0:T(512)}, f32[320]{0:T(512)S(1)}, u32[]{:S(2)}) copy-start(f32[320]{0:T(512)S(1)} %convert_element_type.39) | copy-start | bytes 3844
  47.4 13.4 %copy-start.15 = (f32[128]{0:T(128)S(1)}, f32[128]{0:T(128)}, u32[]{:S(2)}) copy-start(f32[128]{0:T(128)} %param.23) | copy-start | bytes 1540
  47.5 13.5 %copy-start.16 = (f32[128]{0:T(128)S(1)}, f32[128]{0:T(128)}, u32[]{:S(2)}) copy-start(f32[128]{0:T(128)} %param.24) | copy-start | bytes 1540
  47.5 14.2 %copy-start.18 = (s32[5]{0:T(128)S(1)}, s32[5]{0:T(128)}, u32[]{:S(2)}) copy-start(s32[5]{0:T(128)} %param.17) | copy-start | bytes 64
  47.5 14.5 %copy-start.3 = (bf16[128,128]{1,0:T(8,128)(2,1)S(1)}, bf16[128,128]{1,0:T(8,128)(2,1)}, u32[]{:S(2)}) copy-start(bf16[128,128]{1,0:T(8,128)(2,1)} %gate_w_ref.1) | copy-start | bytes 98308
  48.8 33.9 %all-to-all-start = ((bf16[32,4,3200]{2,1,0:T(4,128)(2,1)}), bf16[32,4,3200]{2,1,0:T(4,128)(2,1)}, u32[]{:S(2)}, u32[]{:S(2)}) async-start(bf16[32,4,3200]{2,1,0:T(4,128)(2,1)} %bitcast.32), calls=%async_computation | async-start | bytes 1638400 | tf_op jit(solution)/shard_map/all_to_all | solution.py:509
  61.9 2.1 %copy-start.14 = (f32[320]{0:T(512)S(1)}, f32[320]{0:T(512)}, u32[]{:S(2)}) copy-start(f32[320]{0:T(512)} %copy-done.13) | copy-start | bytes 3844
  62.0 22.3 %copy-start.4 = (bf16[128,128]{1,0:T(8,128)(2,1)S(1)}, bf16[128,128]{1,0:T(8,128)(2,1)}, u32[]{:S(2)}) copy-start(bf16[128,128]{1,0:T(8,128)(2,1)} %out_w_ref.2) | copy-start | bytes 98308
  62.0 22.3 %copy-start.6 = (f32[128]{0:T(128)S(1)}, f32[128]{0:T(128)}, u32[]{:S(2)}) copy-start(f32[128]{0:T(128)} %param.26) | copy-start | bytes 1540
  62.0 22.3 %copy-start.7 = (f32[128]{0:T(128)S(1)}, f32[128]{0:T(128)}, u32[]{:S(2)}) copy-start(f32[128]{0:T(128)} %param.27) | copy-start | bytes 1540
  84.3 0.8 copy-start.1
  85.2 0.7 copy-start.10
  85.8 3.7 %copy-start.2 = (bf16[128,512]{1,0:T(8,128)(2,1)S(1)}, bf16[128,512]{1,0:T(8,128)(2,1)}, u32[]{:S(2)}) copy-start(bf16[128,512]{1,0:T(8,128)(2,1)} %qkvg_ref.1) | copy-start | bytes 393220
  89.6 13.7 %copy-start.11 = (f32[320,320]{1,0:T(8,128)S(1)}, f32[320,320]{1,0:T(8,128)}, u32[]{:S(2)}) copy-start(f32[320,320]{1,0:T(8,128)} %compare_convert_fusion) | copy-start | bytes 1228804
  89.6 13.7 %copy-start.12 = (f32[320]{0:T(512)S(1)}, f32[320]{0:T(512)}, u32[]{:S(2)}) copy-start(f32[320]{0:T(512)} %add_multiply_fusion) | copy-start | bytes 3844
  89.6 13.7 %copy-start.17 = (f32[4]{0:T(128)S(1)}, f32[4]{0:T(128)}, u32[]{:S(2)}) copy-start(f32[4]{0:T(128)} %param.30) | copy-start | bytes 52
  101.8 1.5 %copy-start = (bf16[10,320,384]{2,1,0:T(8,128)(2,1)}, bf16[10,320,384]{2,1,0:T(8,128)(2,1)S(1)}, u32[]{:S(2)}) copy-start(bf16[10,320,384]{2,1,0:T(8,128)(2,1)S(1)} %get-tuple-element.17.qkv_ref) | copy-start | bytes 7372804
  103.6 0.8 copy-start.5

commit v7 on v6

--- a/solution.py
+++ b/solution.py
@@ -254,7 +254,7 @@
 
     for d in range(nq // 2):
         if d == 1:
-            lax.fori_loop(0, columns // 2, project, 0)
+            lax.fori_loop(0, columns // 5, project, 0)
         source = lax.rem(q + nq - 2 * d, nq)
         block = src if d == 0 else out.at[source, r]
         if d > 0:
@@ -266,7 +266,7 @@
             ]
         )
         to_mate.append(send(block, (source, r), mate_send.at[0, d], mate_recv.at[0, d], mate))
-    lax.fori_loop(columns // 2, columns, project, 0)
+    lax.fori_loop(columns // 5, columns, project, 0)
     for d in range(nq // 2):
         source = lax.rem(q + nq - 2 * d, nq)
         for e in range(nr - 1):

time: 123 us -> 123 us (level)
  no operation moved by 1% of the time
where the time goes in v7:
time: 123 us
  Pallas kernels  78.2 us (64%)
  waiting for transfers between devices  17.2 us (14%)
  local copies, waits for them, and re-layouts  12.6 us (10%)
  starting transfers between devices  11.9 us (10%)
  other arithmetic  2.88 us (2%)
    pallas_call x1, Pallas kernels, spread_all(): pl.pallas_call(functools.partial(spread_kernel, nr, nq), out_shape=[jax.S...  37 us
    pallas_call x1, Pallas kernels, attend_and_return(): pl.pallas_call(functools.partial(attention_kernel, nr, columns), grid=(co...  17.5 us
    all_to_all x1, waiting for transfers between devices, on_device(): lax.all_to_all(product, axes, split_axis=0, concat_axis=0, tiled=True)  17.2 us
    pallas_call x1, Pallas kernels, gather_all(): pl.pallas_call(functools.partial(gather_kernel, nr, nq), out_shape=[jax.S...  12.2 us
    all_to_all x1, starting transfers between devices, on_device(): lax.all_to_all(product, axes, split_axis=0, concat_axis=0, tiled=True)  11.9 us
    pallas_call x3, Pallas kernels, step_call(): pl.pallas_call(kernel, grid=(steps,), in_specs=[cut_spec(a.shape, dim, st...  8.8 us
    unnamed x40, local copies, waits for them, and re-layouts  5.55 us
    pallas_call x1, Pallas kernels, on_device(): pl.pallas_call(product_kernel, grid=(col_devices,), in_specs=[cut_spec(sp...  2.62 us
  transfers between devices with their start and end apart: 1, of which 1 were waited for; matrix products, arithmetic and copies ran while one was open for 2% of the time, Pallas kernels for 2%

profile of v7, /device:TPU:0, one launch (start us, length us, event | category | flops | bytes accessed | tf_op | source)
XLA Modules:
  0.0 123.0 jit_solution(5600124036857777777)
XLA Ops:
  0.0 0.7 convert_element_type.38
  1.2 1.3 %copy.42 = bf16[80,40,128]{2,0,1:T(8,128)(2,1)S(1)} copy(bf16[80,40,128]{2,1,0:T(8,128)(2,1)} %param.16) | data formatting | bytes 1638400 | tf_op args[0]
  2.4 1.0 copy.26
  3.5 3.1 %shard_map.154 = bf16[256,3200]{1,0:T(8,128)(2,1)S(1)} custom-call(bf16[40,80,128]{2,1,0:T(8,128)(2,1)S(1)} %bitcast.33, f32[1,3200]{1,0:T(1,128)S(1)} %mul.61.mask_ref, f32[1,128]{1,0:T(1,128)S(1)} %bitcast.44, f32[1,128]{1,0:T(1,128)S(1)} %bitcast.46, bf16[512,128]{1,0:T(8,128)(2,1)S(1)} %bitcast.39), custom_call_target="tpu_custom_call" | custom-call | tf_op jit(solution)/shard_map/pallas_call | solution.py:391
  6.6 37.0 %shard_map.155 = (bf16[32,8,3200]{2,1,0:T(8,128)(2,1)S(1)}, bf16[10,4,80,128]{3,2,1,0:T(8,128)(2,1)S(1)}) custom-call(bf16[32,8,3200]{2,1,0:T(8,128)(2,1)S(1)} %bitcast.35, bf16[4,10,80,128]{3,2,1,0:T(8,128)(2,1)S(1)} %bitcast.34), custom_call_target="tpu_custom_call" | custom-call | tf_op jit(solution)/shard_map/pallas_call | solution.py:364
  43.7 2.6 %shard_map.156 = bf16[4,320,320]{2,1,0:T(8,128)(2,1)S(1)} custom-call(bf16[32,8,3200]{2,1,0:T(8,128)(2,1)S(1)} %get-tuple-element.13.spread_ref), custom_call_target="tpu_custom_call" | custom-call | tf_op jit(solution)/shard_map/pallas_call | solution.py:499
  46.3 1.1 reshape.112
  47.5 1.3 %copy.41 = bf16[4,32,3200]{2,0,1:T(4,128)(2,1)} copy(bf16[4,32,3200]{2,1,0:T(8,128)(2,1)S(1)} %reshape.112) | data formatting | bytes 1638400 | tf_op jit(solution)/shard_map/reshape | solution.py:508
  48.8 11.9 %all-to-all-start = ((bf16[32,4,3200]{2,1,0:T(4,128)(2,1)}), bf16[32,4,3200]{2,1,0:T(4,128)(2,1)}, u32[]{:S(2)}, u32[]{:S(2)}) async-start(bf16[32,4,3200]{2,1,0:T(4,128)(2,1)} %bitcast.32), calls=%async_computation | async-start | bytes 1638400 | tf_op jit(solution)/shard_map/all_to_all | solution.py:509
  61.0 0.7 copy.30.out_shift_ref
  62.0 2.0 %shard_map.157.gate_ref = f32[10,320,128]{2,1,0:T(8,128)S(1)} custom-call(bf16[10,320,128]{2,1,0:T(8,128)(2,1)S(1)} %bitcast.36, f32[1,128]{1,0:T(1,128)S(1)} %bitcast.45, f32[1,128]{1,0:T(1,128)S(1)} %bitcast.47, bf16[128,128]{1,0:T(8,128)(2,1)S(1)} %copy-done.3), custom_call_target="tpu_custom_call" | custom-call | tf_op jit(solution)/shard_map/pallas_call | solution.py:391
  64.0 0.6 add_multiply_fusion
  64.6 0.9 compare_convert_fusion
  65.5 17.2 %all-to-all-done = bf16[32,4,3200]{2,1,0:T(4,128)(2,1)} async-done(((bf16[32,4,3200]{2,1,0:T(4,128)(2,1)}), bf16[32,4,3200]{2,1,0:T(4,128)(2,1)}, u32[]{:S(2)}, u32[]{:S(2)}) %all-to-all-start) | async-done | bytes 819232 | tf_op jit(solution)/shard_map/all_to_all | solution.py:509
  82.7 1.6 %reshape.113.product_ref = bf16[128,3200]{1,0:T(8,128)(2,1)S(1)} reshape(bf16[32,4,3200]{2,1,0:T(4,128)(2,1)} %all-to-all-done) | data formatting | bytes 1638400 | tf_op jit(solution)/shard_map/reshape | solution.py:515
  84.3 0.8 copy-done.1
  85.2 0.7 copy-done.10
  85.8 3.7 %shard_map.158 = (bf16[10,320,128]{2,1,0:T(8,128)(2,1)S(1)}, bf16[10,4,320]{2,1,0:T(4,128)(2,1)S(1)}) custom-call(bf16[10,320,128]{2,1,0:T(8,128)(2,1)S(1)} %bitcast.37, bf16[128,3200]{1,0:T(8,128)(2,1)S(1)} %reshape.113.product_ref, f32[10,320,128]{2,1,0:T(8,128)S(1)} %shard_map.157.gate_ref, f32[128,1]{1,0:T(8,128)S(1)} %copy.29.out_gain_ref, ...), custom_call_target="tpu_custom_call" | custom-call | tf_op jit(solution)/shard_map/pallas_call | solution.py:391
  89.6 12.2 %shard_map.159 = (bf16[8,4,10,4,320]{4,3,2,1,0:T(4,128)(2,1)S(1)}, bf16[10,320,384]{2,1,0:T(8,128)(2,1)S(1)}, f32[10,320,128]{2,1,0:T(8,128)S(1)}) custom-call(bf16[10,4,320]{2,1,0:T(4,128)(2,1)S(1)} %get-tuple-element.15.src, bf16[10,320,128]{2,1,0:T(8,128)(2,1)S(1)} %get-tuple-element.14.mid_ref, f32[1,128]{1,0:T(1,128)S(1)} %bitcast.41, ...), custom_call_target="tpu_custom_call" | custom-call | tf_op jit(solution)/shard_map/pallas_call | solution.py:293
  101.8 0.4 bitcast_convert_fusion
  102.2 1.1 copy-done
  103.7 0.6 copy-done.5
  104.3 17.5 %shard_map.160 = bf16[4,10,80,128]{3,2,1,0:T(8,128)(2,1)S(1)} custom-call(bf16[10,320,128]{2,1,0:T(8,128)(2,1)S(1)} %get-tuple-element.14.mid_ref, f32[4,320,384]{2,1,0:T(8,128)S(1)} %pad.4.extra_ref, f32[320,1]{1,0:T(8,128)S(1)} %convert_element_type.47.valid_i_ref, f32[10,1,1]{2,1,0:T(1,128)S(1)} %copy.33.valid_j_ref, bf16[10,320,384]{2,1,0:T(8,128)(2,1)} %copy-done, ...), custom_call_target="tpu_custom_call" | custom-call | tf_op jit(solution)/shard_map/pallas_call | solution.py:404
  121.9 1.1 copy.40
  (49 shorter events, 1.6 us)
Async XLA Ops:
  0.0 3.5 %copy-start.8 = (f32[128]{0:T(128)S(1)}, f32[128]{0:T(128)}, u32[]{:S(2)}) copy-start(f32[128]{0:T(128)} %param.19) | copy-start | bytes 1540
  0.0 3.5 %copy-start.9 = (f32[128]{0:T(128)S(1)}, f32[128]{0:T(128)}, u32[]{:S(2)}) copy-start(f32[128]{0:T(128)} %param.20) | copy-start | bytes 1540
  0.8 61.0 %copy-start.13 = (f32[320]{0:T(512)}, f32[320]{0:T(512)S(1)}, u32[]{:S(2)}) copy-start(f32[320]{0:T(512)S(1)} %convert_element_type.39) | copy-start | bytes 3844
  47.4 13.4 %copy-start.15 = (f32[128]{0:T(128)S(1)}, f32[128]{0:T(128)}, u32[]{:S(2)}) copy-start(f32[128]{0:T(128)} %param.23) | copy-start | bytes 1540
  47.5 13.5 %copy-start.16 = (f32[128]{0:T(128)S(1)}, f32[128]{0:T(128)}, u32[]{:S(2)}) copy-start(f32[128]{0:T(128)} %param.24) | copy-start | bytes 1540
  47.5 14.2 %copy-start.18 = (s32[5]{0:T(128)S(1)}, s32[5]{0:T(128)}, u32[]{:S(2)}) copy-start(s32[5]{0:T(128)} %param.17) | copy-start | bytes 64
  47.5 14.5 %copy-start.3 = (bf16[128,128]{1,0:T(8,128)(2,1)S(1)}, bf16[128,128]{1,0:T(8,128)(2,1)}, u32[]{:S(2)}) copy-start(bf16[128,128]{1,0:T(8,128)(2,1)} %gate_w_ref.1) | copy-start | bytes 98308
  48.8 33.9 %all-to-all-start = ((bf16[32,4,3200]{2,1,0:T(4,128)(2,1)}), bf16[32,4,3200]{2,1,0:T(4,128)(2,1)}, u32[]{:S(2)}, u32[]{:S(2)}) async-start(bf16[32,4,3200]{2,1,0:T(4,128)(2,1)} %bitcast.32), calls=%async_computation | async-start | bytes 1638400 | tf_op jit(solution)/shard_map/all_to_all | solution.py:509
  61.9 2.1 %copy-start.14 = (f32[320]{0:T(512)S(1)}, f32[320]{0:T(512)}, u32[]{:S(2)}) copy-start(f32[320]{0:T(512)} %copy-done.13) | copy-start | bytes 3844
  62.0 22.3 %copy-start.4 = (bf16[128,128]{1,0:T(8,128)(2,1)S(1)}, bf16[128,128]{1,0:T(8,128)(2,1)}, u32[]{:S(2)}) copy-start(bf16[128,128]{1,0:T(8,128)(2,1)} %out_w_ref.2) | copy-start | bytes 98308
  62.0 22.3 %copy-start.6 = (f32[128]{0:T(128)S(1)}, f32[128]{0:T(128)}, u32[]{:S(2)}) copy-start(f32[128]{0:T(128)} %param.26) | copy-start | bytes 1540
  62.0 22.3 %copy-start.7 = (f32[128]{0:T(128)S(1)}, f32[128]{0:T(128)}, u32[]{:S(2)}) copy-start(f32[128]{0:T(128)} %param.27) | copy-start | bytes 1540
  84.3 0.8 copy-start.1
  85.2 0.7 copy-start.10
  85.8 3.7 %copy-start.2 = (bf16[128,512]{1,0:T(8,128)(2,1)S(1)}, bf16[128,512]{1,0:T(8,128)(2,1)}, u32[]{:S(2)}) copy-start(bf16[128,512]{1,0:T(8,128)(2,1)} %qkvg_ref.1) | copy-start | bytes 393220
  89.6 13.7 %copy-start.11 = (f32[320,320]{1,0:T(8,128)S(1)}, f32[320,320]{1,0:T(8,128)}, u32[]{:S(2)}) copy-start(f32[320,320]{1,0:T(8,128)} %compare_convert_fusion) | copy-start | bytes 1228804
  89.6 13.7 %copy-start.12 = (f32[320]{0:T(512)S(1)}, f32[320]{0:T(512)}, u32[]{:S(2)}) copy-start(f32[320]{0:T(512)} %add_multiply_fusion) | copy-start | bytes 3844
  89.6 13.7 %copy-start.17 = (f32[4]{0:T(128)S(1)}, f32[4]{0:T(128)}, u32[]{:S(2)}) copy-start(f32[4]{0:T(128)} %param.30) | copy-start | bytes 52
  101.8 1.5 %copy-start = (bf16[10,320,384]{2,1,0:T(8,128)(2,1)}, bf16[10,320,384]{2,1,0:T(8,128)(2,1)S(1)}, u32[]{:S(2)}) copy-start(bf16[10,320,384]{2,1,0:T(8,128)(2,1)S(1)} %get-tuple-element.17.qkv_ref) | copy-start | bytes 7372804
  103.6 0.8 copy-start.5
